TPU v7x, 32 devices: a whole 2x2x4 slice. The times are simulated.
32 devices in a mesh: dp: 4 (over y, x), shard: 8 (over z, core).
Axes of the slice: x: 2, y: 2, z: 4, core: 2. Of those that a mesh axis runs over, the one named last changes fastest.
Arguments:
- activations: bfloat16 [32, 256, 1024], P(('dp', 'shard')), may hold values from -120 to 120
- out_grad: bfloat16 [32, 256, 1024], P(('dp', 'shard')), may hold values from -6 to 6
- weights: bfloat16 [256, 27, 256], P('shard'), may hold values from -0.078125 to 0.078125
Outputs:
- activated: bfloat16 [32, 256, 1024], P(('dp', 'shard'))
- update: float32 [256, 27, 256], P('shard')
All inputs are finite; a program needn't handle non-finite values.
Results may differ from a plain program's by a relative error of at most 0.0026.
Values may be sent and summed in bfloat16 or wider, within the bound.
No kernel may reach another device: no remote copies, remote signals or barrier semaphores. Data moves between devices by JAX's collectives and lax.ppermute only.
A program may use at most 128 MiB of HBM per device.

v0:
```python
import functools
import math

import jax
import jax.numpy as jnp
from jax import lax
from jax.experimental import pallas as pl
from jax.experimental.pallas import tpu as pltpu
from jax.sharding import PartitionSpec as P

SX = 4
SY = 16
SZ = 16
NS_ITERS = 8
DAMPING = 0.001
AXES = ("dp", "shard")
NT = (((1,), (1,)), ((), ()))
VMEM = pl.BlockSpec(memory_space=pltpu.VMEM)
SMEM = pl.BlockSpec(memory_space=pltpu.SMEM)
PARAMS = pltpu.CompilerParams(vmem_limit_bytes=32 * 1024 * 1024)


def exchange(x, planes, pairs, dp=0, z=0, core=0):
    perm = []
    for a in range(planes):
        for b in range(pairs):
            for c in range(2):
                here = (a * pairs + b) * 2 + c
                there = ((a ^ dp) * pairs + (b ^ z)) * 2 + (c ^ core)
                perm.append((here, there))
    return lax.ppermute(x, AXES, perm)


def after(x, *others):
    return lax.optimization_barrier((x, *others))[0]


def rows_of(x, index, height):
    return lax.dynamic_slice_in_dim(x, index * height, height, 0)


def place(buffer, block, index):
    return lax.dynamic_update_slice_in_dim(buffer, block, index * block.shape[0], 0)


def by_core(core, mine, other):
    return jnp.where(
        core == 0, jnp.concatenate([mine, other]), jnp.concatenate([other, mine])
    )


def dot3(left, right):
    left_high = left.astype(jnp.bfloat16)
    left_low = (left - left_high.astype(jnp.float32)).astype(jnp.bfloat16)
    right_high = right.astype(jnp.bfloat16)
    right_low = (right - right_high.astype(jnp.float32)).astype(jnp.bfloat16)

    def dot(a, b):
        return jnp.dot(a, b, preferred_element_type=jnp.float32)

    return dot(left_high, right_high) + (dot(left_high, right_low) + dot(left_low, right_high))


def shifter(shape):
    cells = shape[1]
    lane = lax.broadcasted_iota(jnp.int32, shape, 1)
    spots = (lane // (SY * SZ), lane // SZ % SY, lane % SZ)
    strides = (SY * SZ, SZ, 1)
    sizes = (SX, SY, SZ)

    def shifted(value, dim, step):
        if step == 0:
            return value
        rolled = pltpu.roll(value, (-step * strides[dim]) % cells, 1)
        inside = spots[dim] < sizes[dim] - 1 if step > 0 else spots[dim] > 0
        return jnp.where(inside, rolled, 0.0)

    return shifted


def columns_kernel(pairs, at, *refs):
    blocks, (result, rows) = refs[:pairs], refs[pairs:]
    height = blocks[0].shape[0]
    for step in range(pairs):
        start = pl.multiple_of((at[0] ^ step) * height, height)
        rows[pl.ds(start, height), :] = blocks[step][...].astype(jnp.float32)
    result[...] = rows[...].T.astype(jnp.bfloat16)


def forward_kernel(taps, out, parts, core, kernel, *refs):
    windows = (refs[:parts], refs[parts : 2 * parts])
    results, (inputs, wide) = refs[2 * parts : -2], refs[-2:]
    slope_out = results[0]
    act_out = results[0].at[2 * out :] if len(results) == 1 else results[1]
    channels, cells = inputs.shape[1:]
    shifted = shifter((out, cells))
    for window, pieces in enumerate(windows):
        cot = gather_window(channels, out, core, pieces, inputs.at[window])
        wide[...] = jnp.dot(kernel[...], inputs[window], preferred_element_type=jnp.float32)
        outputs = None
        for a in range(3):
            over_b = None
            for b in range(3):
                over_c = None
                for c in range(3):
                    tap = 9 * a + 3 * b + c
                    part = shifted(wide[tap * out : (tap + 1) * out, :], 2, c - 1)
                    over_c = part if over_c is None else over_c + part
                part = shifted(over_c, 1, b - 1)
                over_b = part if over_b is None else over_b + part
            part = shifted(over_b, 0, a - 1)
            outputs = part if outputs is None else outputs + part
        sigma = jax.nn.sigmoid(outputs)
        cot = cot.astype(jnp.float32)
        act_out[window * out : (window + 1) * out, :] = (outputs * sigma).astype(jnp.bfloat16)
        slope_out[window * out : (window + 1) * out, :] = (
            cot * sigma * (1.0 + outputs * (1.0 - sigma))
        ).astype(jnp.bfloat16)


def gather_window(channels, out, core, pieces, inputs):
    start = 0
    for piece in pieces:
        height = min(piece.shape[0], channels - start)
        if height > 0:
            inputs[start : start + height, :] = piece[:height, :]
            start += height
    last = pieces[-1]
    first = pl.multiple_of(last.shape[0] - 2 * out + core[0] * out, out)
    return last[pl.ds(first, out), :]


def gradient_kernel(first, taps, out, slopes, inputs, *refs):
    total_in = None if first else refs[0]
    total, moved = refs[-2:]
    channels, cells = inputs.shape[1:]
    shifted = shifter((out, cells))
    for window in range(2):
        slope = slopes[window * out : (window + 1) * out, :].astype(jnp.float32)
        for a in range(3):
            at_a = shifted(slope, 0, 1 - a)
            for b in range(3):
                at_b = shifted(at_a, 1, 1 - b)
                for c in range(3):
                    tap = 9 * a + 3 * b + c
                    moved[tap * out : (tap + 1) * out, :] = shifted(at_b, 2, 1 - c).astype(
                        jnp.bfloat16
                    )
        sums = lax.dot_general(
            moved[...], inputs[window], NT, preferred_element_type=jnp.float32
        )
        if window == 0:
            total[...] = sums if first else total_in[...] + sums
        else:
            total[...] += sums


def gram_kernel(planes, out, at, core, *refs):
    mine, theirs, (result, slopes) = refs[:planes], refs[planes : 2 * planes], refs[2 * planes :]
    half = result.shape[0]
    cells = mine[0].shape[1]
    own = pl.multiple_of(core[0] * half, half)
    other = pl.multiple_of((1 - core[0]) * half, half)
    for step in range(planes):
        plane = (at[0] ^ step) * out
        for window in range(2):
            columns = slice(window * cells, (window + 1) * cells)
            rows = slice(window * out, (window + 1) * out)
            slopes[pl.ds(pl.multiple_of(own + plane, out), out), columns] = mine[step][rows, :]
            rows = slice((1 - window) * out, (2 - window) * out)
            slopes[pl.ds(pl.multiple_of(other + plane, out), out), columns] = theirs[step][rows, :]
    result[...] = lax.dot_general(
        slopes[pl.ds(own, half), :], slopes[...], NT, preferred_element_type=jnp.float32
    )


def inputs_gram_kernel(core, mine, theirs, result):
    half, channels = result.shape
    own = pl.multiple_of(core[0] * half, half)
    result[...] = lax.dot_general(
        mine[pl.ds(own, half), :], mine[:channels, :], NT, preferred_element_type=jnp.float32
    ) + lax.dot_general(
        theirs[pl.ds(own, half), :], theirs[:channels, :], NT, preferred_element_type=jnp.float32
    )


def sort_kernel(planes, out, at, core, *refs):
    mine, theirs, result = refs[:planes], refs[planes:-1], refs[-1]
    half = result.shape[0] // 2
    for step in range(planes):
        plane = (at[0] ^ step) * out
        piece = mine[step]
        first = piece.shape[0] - 2 * out
        start = pl.multiple_of(core[0] * half + plane, out)
        result[pl.ds(start, out), :] = piece[first : first + out, :]
        start = pl.multiple_of((1 - core[0]) * half + plane, out)
        result[pl.ds(start, out), :] = theirs[step][first + out : first + 2 * out, :]


def newton_kernel(count, core, mine, theirs, result, matrix, both):
    half, size = mine.shape
    matrix[pl.ds(pl.multiple_of(core[0] * half, half), half), :] = mine[...]
    matrix[pl.ds(pl.multiple_of((1 - core[0]) * half, half), half), :] = theirs[...]
    row = lax.broadcasted_iota(jnp.int32, (size, size), 0)
    column = lax.broadcasted_iota(jnp.int32, (size, size), 1)
    identity = jnp.where(row == column, 1.0, 0.0)
    factor = matrix[...] / count + DAMPING * identity
    diagonal = jnp.sum(factor * identity, axis=1, keepdims=True)
    scale = 1.0 / jnp.sum(diagonal, axis=0, keepdims=True)
    error = identity - factor * scale
    both[:size, :] = (identity + error) * scale
    both[size:, :] = error
    for sweep in range(1, NS_ITERS):
        if sweep == 1:
            both[size:, :] = dot3(error, error)
        last = sweep == NS_ITERS - 1
        products = dot3(both[:size, :] if last else both[...], both[size:, :])
        both[:size, :] += products[:size]
        if not last:
            both[size:, :] = products[size:]
    result[...] = both[:size, :]


def update_kernel(planes, taps, out, scale, at, inverse, *refs):
    pieces, (result, rows, factor) = refs[:planes], refs[planes:]
    own_rows = pieces[0].shape[0] // 2
    half = inverse.shape[0] // 2
    for step in range(planes):
        for core in range(2):
            block = (step * 2 + core) * out
            start = pl.multiple_of(core * half + (at[0] ^ step) * out, out)
            factor[block : block + out, :] = inverse[pl.ds(start, out), :]
            for tap in range(taps):
                rows[tap * own_rows : (tap + 1) * own_rows, block : block + out] = pieces[step][
                    core * own_rows : (core + 1) * own_rows, tap * out : (tap + 1) * out
                ]
    result[...] = dot3(rows[...], factor[...]) * scale


def call(kernel, args, shapes, scratch, flops, scalars=0, aliases=None):
    moved = sum(a.size * a.dtype.itemsize for a in list(args) + list(shapes))
    return pl.pallas_call(
        kernel,
        out_shape=tuple(shapes),
        in_specs=[SMEM] * scalars + [VMEM] * (len(args) - scalars),
        out_specs=tuple([VMEM] * len(shapes)),
        scratch_shapes=scratch,
        input_output_aliases=aliases or {},
        compiler_params=PARAMS,
        cost_estimate=pl.CostEstimate(flops=flops, bytes_accessed=moved, transcendentals=0),
    )(*args)


def shards(planes, pairs, activations, out_grad, weights):
    f32, bf16 = jnp.float32, jnp.bfloat16
    shape = jax.ShapeDtypeStruct
    inputs = activations[0]
    cotangent = out_grad[0]
    channels, cells = inputs.shape
    own_rows, taps, _ = weights.shape
    out = channels // (2 * planes)
    half = channels // 2
    wide = taps * out
    my_plane = lax.axis_index("dp")
    my_index = lax.axis_index("shard")
    my_pair = my_index // 2
    my_core = my_index % 2
    at_plane = my_plane.reshape(1)
    at_pair = my_pair.reshape(1)
    at_core = my_core.reshape(1)
    swap = functools.partial(exchange, planes=planes, pairs=pairs)

    def kernel_columns(core):
        start = core * half + my_plane * out
        part = lax.dynamic_slice_in_dim(weights, start, out, 2)
        return part.reshape(own_rows, wide)

    def cotangent_rows(step):
        plane = my_plane ^ step
        first = rows_of(cotangent, plane, out)
        second = lax.dynamic_slice_in_dim(cotangent, half + plane * out, out, 0)
        return [first, second]

    block = by_core(my_core, kernel_columns(my_core), swap(kernel_columns(1 - my_core), core=1))
    blocks = [block] + [swap(block, z=step) for step in range(1, pairs)]
    (kernel,) = call(
        functools.partial(columns_kernel, pairs),
        (at_pair, *blocks),
        [shape((wide, channels), bf16)],
        [pltpu.VMEM((channels, wide), f32)],
        0,
        scalars=1,
    )

    own = jnp.concatenate([inputs, *cotangent_rows(0)])
    straight = [step for step in range(1, planes) if step & (step - 1) == 0]
    arrived = [
        swap(jnp.concatenate([inputs, *cotangent_rows(step)]), dp=step) for step in straight
    ]
    arrived = lax.optimization_barrier(tuple(arrived))
    windows = {0: [own], **{step: [part] for step, part in zip(straight, arrived)}}
    for step in range(1, planes):
        if step not in windows:
            low = step & -step
            high = (step ^ low) & -(step ^ low)
            by_high = windows[step ^ high]
            by_low = windows[step ^ low]
            first = by_high[0] if len(by_high) == 3 else by_high[0][:half]
            second = by_low[1] if len(by_low) == 3 else by_low[0][half:channels]
            cot = swap(jnp.concatenate(cotangent_rows(step)), dp=step)
            windows[step] = [swap(first, dp=high), swap(second, dp=low), cot]

    others = swap(own, core=1)
    (part,) = call(
        inputs_gram_kernel,
        (at_core, own, others),
        [shape((half, channels), f32)],
        [],
        2 * 2 * half * channels * cells,
        scalars=1,
    )
    part = after(part, *blocks)
    a_half = part
    for step in range(1, pairs):
        a_half = a_half + swap(part, z=step)

    total = None
    back = []
    theirs = []
    slope = None
    for step in range(planes):
        mine = windows[step]
        last = step == planes - 1
        if step > 0:
            tied = (slope, a_half) if last else (slope,)
            mine = [after(part, *tied) for part in mine]
            others = [swap(part, core=1) for part in mine]
        else:
            others = [others]
        heights = (2 * out, 2 * out) if last else (4 * out,)
        *results, pair = call(
            functools.partial(forward_kernel, taps, out, len(mine)),
            (at_core, kernel, *mine, *others),
            [shape((height, cells), bf16) for height in heights]
            + [shape((2, channels, cells), bf16)],
            [pltpu.VMEM((wide, cells), f32)],
            2 * 2 * wide * channels * cells,
            scalars=1,
        )
        slope = results[0]
        back.append(slope if step == 0 else swap(slope, dp=step))
        theirs.append(swap(back[-1], core=1))
        (total,) = call(
            functools.partial(gradient_kernel, step == 0, taps, out),
            (slope, pair) + (() if step == 0 else (total,)),
            [shape((wide, channels), f32)],
            [pltpu.VMEM((wide, cells), bf16)],
            2 * 2 * wide * channels * cells,
            aliases={} if step == 0 else {2: 0},
        )
    part = after(a_half, *windows[planes - 1])
    a_half = part
    for step in range(1, planes):
        a_half = a_half + swap(part, dp=step)

    count = planes * pairs * 2 * cells

    def inverse_of(mine):
        return call(
            functools.partial(newton_kernel, count),
            (at_core, mine, swap(mine, core=1)),
            [shape((channels, channels), f32)],
            [pltpu.VMEM((channels, channels), f32), pltpu.VMEM((2 * channels, channels), f32)],
            6 * NS_ITERS * 4 * channels**3,
            scalars=1,
        )[0]

    (g_half,) = call(
        functools.partial(gram_kernel, planes, out),
        (at_plane, at_core, *back, *theirs),
        [shape((half, channels), f32)],
        [pltpu.VMEM((channels, 2 * cells), bf16)],
        2 * 2 * half * channels * cells,
        scalars=2,
    )
    part = rows_of(g_half, my_plane, out)
    for step in range(1, planes):
        part = part + swap(rows_of(g_half, my_plane ^ step, out), dp=step)
    over_z = part
    for step in range(1, pairs):
        over_z = over_z + swap(part, z=step)
    g_half = jnp.zeros((half, channels), f32)
    for step in range(planes):
        part = over_z if step == 0 else swap(over_z, dp=step)
        g_half = place(g_half, part, my_plane ^ step)

    inv_a = inverse_of(a_half)
    inv_g = inverse_of(g_half)

    product = lax.dot_general(inv_a, total, NT, precision=lax.Precision.HIGHEST)
    narrow = product.astype(bf16)
    rows = rows_of(product, my_pair, 2 * own_rows)
    for step in range(1, pairs):
        part = swap(rows_of(narrow, my_pair ^ step, 2 * own_rows), z=step)
        rows = rows + part.astype(f32)
    mine = rows_of(rows, my_core, own_rows)
    other = swap(rows_of(rows, 1 - my_core, own_rows), core=1)
    block = by_core(my_core, mine, other)
    pieces = [block] + [swap(block, dp=step) for step in range(1, planes)]
    (update,) = call(
        functools.partial(update_kernel, planes, taps, out, 1.0 / math.sqrt(count)),
        (at_plane, inv_g, *pieces),
        [shape((taps * own_rows, channels), f32)],
        [pltpu.VMEM((taps * own_rows, channels), f32), pltpu.VMEM((channels, channels), f32)],
        6 * 2 * taps * own_rows * channels**2,
        scalars=1,
    )
    update = update.reshape(taps, own_rows, channels).transpose(1, 0, 2)

    last = results[1]
    last = swap(after(last, over_z), dp=planes - 1)
    mine = [*back[:-1], last]
    theirs = [*theirs[:-1], swap(last, core=1)]
    (activated,) = call(
        functools.partial(sort_kernel, planes, out),
        (at_plane, at_core, *mine, *theirs),
        [shape((channels, cells), bf16)],
        [],
        0,
        scalars=2,
    )
    return activated[None], update


def solution(mesh):
    planes = mesh.shape["dp"]
    pairs = mesh.shape["shard"] // 2
    return jax.shard_map(
        functools.partial(shards, planes, pairs),
        mesh=mesh,
        in_specs=(
            P(("dp", "shard"), None, None),
            P(("dp", "shard"), None, None),
            P("shard", None, None),
        ),
        out_specs=(P(("dp", "shard"), None, None), P("shard", None, None)),
        check_vma=False,
    )
```

profile of v0, /device:TPU:0, one launch (start us, length us, event | category | flops | bytes accessed | tf_op | source)
XLA Modules:
  0.0 127.9 jit_solution(8919193649706699761)
XLA Ops:
  3.9 3.0 %collective-permute-start.6 = (bf16[320,1024]{1,0:T(8,128)(2,1)}, bf16[320,1024]{1,0:T(8,128)(2,1)S(1)}, u32[]{:S(2)}, u32[]{:S(2)}) collective-permute-start(bf16[320,1024]{1,0:T(8,128)(2,1)} %get-tuple-element.50), channel_id=1, source_target_pairs={{0,16},{1,17},{2,18},{3,19},{4,20},{5,21},{6,22},{7,23},{8,24},{9,... | collective-permute-start | bytes 1966088 | tf_op jit(solution)/shard_map/ppermute | solution.py:31
  11.4 3.7 %collective-permute-start.3 = (bf16[64,864]{1,0:T(8,128)(2,1)S(1)}, bf16[64,864]{1,0:T(8,128)(2,1)S(1)}, u32[]{:S(2)}, u32[]{:S(2)}) collective-permute-start(bf16[64,864]{1,0:T(8,128)(2,1)S(1)} %maximum_select_fusion.1.refs_0_), channel_id=1, source_target_pairs={{0,6},{1,7},{2,4},{3,5},{4,2},{5,3},{6,0},{7,1},{8,14},{9,15},{10,... | collective-permute-start | bytes 331784 | tf_op jit(solution)/shard_map/ppermute | solution.py:31
  15.1 4.2 %collective-permute-done.3.refs_3_ = bf16[64,864]{1,0:T(8,128)(2,1)S(1)} collective-permute-done((bf16[64,864]{1,0:T(8,128)(2,1)S(1)}, bf16[64,864]{1,0:T(8,128)(2,1)S(1)}, u32[]{:S(2)}, u32[]{:S(2)}) %collective-permute-start.3) | collective-permute-done | bytes 110624 | tf_op jit(solution)/shard_map/ppermute | solution.py:31
  19.3 4.6 %collective-permute-start.1 = (bf16[64,864]{1,0:T(8,128)(2,1)S(1)}, bf16[64,864]{1,0:T(8,128)(2,1)S(1)}, u32[]{:S(2)}, u32[]{:S(2)}) collective-permute-start(bf16[64,864]{1,0:T(8,128)(2,1)S(1)} %maximum_select_fusion.1.refs_0_), channel_id=1, source_target_pairs={{0,2},{1,3},{2,0},{3,1},{4,6},{5,7},{6,4},{7,5},{8,10},{9,11},{10,... | collective-permute-start | bytes 331784 | tf_op jit(solution)/shard_map/ppermute | solution.py:31
  25.4 2.4 %collective-permute-done.1.refs_1_ = bf16[64,864]{1,0:T(8,128)(2,1)S(1)} collective-permute-done((bf16[64,864]{1,0:T(8,128)(2,1)S(1)}, bf16[64,864]{1,0:T(8,128)(2,1)S(1)}, u32[]{:S(2)}, u32[]{:S(2)}) %collective-permute-start.1) | collective-permute-done | bytes 110624 | tf_op jit(solution)/shard_map/ppermute | solution.py:31
  28.0 2.1 %shard_map.51 = (bf16[128,1024]{1,0:T(8,128)(2,1)S(1)}, bf16[2,256,1024]{2,1,0:T(8,128)(2,1)S(1)}) custom-call(s32[1]{0:T(128)} %bitcast.1.core, bf16[864,256]{1,0:T(8,128)(2,1)S(1)} %shard_map.50.kernel, bf16[320,1024]{1,0:T(8,128)(2,1)S(1)} %get-tuple-element.52.refs_0_.mine, bf16[320,1024]{1,0:T(8,128)(2,1)S(1)} %collective-permute-done.4.refs_1_.theirs), custom_call_target="tpu_custom_call" | custom-call | flops 905969664 | bytes 3063812 | tf_op jit(solution)/shard_map/pallas_call | solution.py:242
  37.3 2.8 %shard_map.52 = (bf16[128,1024]{1,0:T(8,128)(2,1)}, bf16[2,256,1024]{2,1,0:T(8,128)(2,1)S(1)}) custom-call(s32[1]{0:T(128)} %bitcast.1.core, bf16[864,256]{1,0:T(8,128)(2,1)S(1)} %shard_map.50.kernel, bf16[320,1024]{1,0:T(8,128)(2,1)S(1)} %collective-permute-done.5.refs_0_, bf16[320,1024]{1,0:T(8,128)(2,1)S(1)} %collective-permute-done.7.refs_1_), custom_call_target="tpu_custom_call" | custom-call | flops 905969664 | bytes 3063812 | tf_op jit(solution)/shard_map/pallas_call | solution.py:242
  41.1 2.4 %collective-permute-start.16 = (bf16[64,1024]{1,0:T(8,128)(2,1)S(1)}, bf16[64,1024]{1,0:T(8,128)(2,1)S(1)}, u32[]{:S(2)}, u32[]{:S(2)}) collective-permute-start(bf16[64,1024]{1,0:T(8,128)(2,1)S(1)} %pad_maximum_fusion.3), channel_id=1, source_target_pairs={{0,24},{1,25},{2,26},{3,27},{4,28},{5,29},{6,30},{7,31},{8,16},{9,... | collective-permute-start | bytes 393224 | tf_op jit(solution)/shard_map/ppermute | solution.py:31
  43.6 2.9 %collective-permute-done.13 = f32[128,256]{1,0:T(8,128)S(1)} collective-permute-done((f32[128,256]{1,0:T(8,128)S(1)}, f32[128,256]{1,0:T(8,128)S(1)}, u32[]{:S(2)}, u32[]{:S(2)}) %collective-permute-start.13) | collective-permute-done | bytes 131104 | tf_op jit(solution)/shard_map/ppermute | solution.py:31
  47.3 2.1 %collective-permute-start.39 = (f32[128,256]{1,0:T(8,128)S(1)}, f32[128,256]{1,0:T(8,128)S(1)}, u32[]{:S(2)}, u32[]{:S(2)}) collective-permute-start(f32[128,256]{1,0:T(8,128)S(1)} %add_add_fusion.1), channel_id=1, source_target_pairs={{0,24},{1,25},{2,26},{3,27},{4,28},{5,29},{6,30},{7,31},{8,16},{9,... | collective-permute-start | bytes 393224 | tf_op jit(solution)/shard_map/ppermute | solution.py:31
  50.8 3.8 %collective-permute-done.39 = f32[128,256]{1,0:T(8,128)S(1)} collective-permute-done((f32[128,256]{1,0:T(8,128)S(1)}, f32[128,256]{1,0:T(8,128)S(1)}, u32[]{:S(2)}, u32[]{:S(2)}) %collective-permute-start.39) | collective-permute-done | bytes 131104 | tf_op jit(solution)/shard_map/ppermute | solution.py:31
  56.9 2.1 %shard_map.60.refs_0_ = f32[864,256]{1,0:T(8,128)S(1)} custom-call(bf16[128,1024]{1,0:T(8,128)(2,1)S(1)} %get-tuple-element.21.refs_0_.slopes, bf16[2,256,1024]{2,1,0:T(8,128)(2,1)S(1)} %copy-done.3), custom_call_target="tpu_custom_call" | custom-call | flops 905969664 | bytes 2195456 | tf_op jit(solution)/shard_map/pallas_call | solution.py:242
  60.4 2.1 %shard_map.53 = (bf16[128,1024]{1,0:T(8,128)(2,1)S(1)}, bf16[2,256,1024]{2,1,0:T(8,128)(2,1)S(1)}) custom-call(s32[1]{0:T(128)} %bitcast.1.core, bf16[864,256]{1,0:T(8,128)(2,1)S(1)} %shard_map.50.kernel, bf16[320,1024]{1,0:T(8,128)(2,1)S(1)} %collective-permute-done.6.refs_0_, bf16[320,1024]{1,0:T(8,128)(2,1)S(1)} %collective-permute-done.9.refs_1_), custom_call_target="tpu_custom_call" | custom-call | flops 905969664 | bytes 3063812 | tf_op jit(solution)/shard_map/pallas_call | solution.py:242
  63.7 4.1 %shard_map.59 = f32[256,256]{1,0:T(8,128)S(1)} custom-call(s32[1]{0:T(128)} %bitcast.1.core, f32[128,256]{1,0:T(8,128)S(1)} %add_add_fusion.mine, f32[128,256]{1,0:T(8,128)S(1)} %collective-permute-done.40.theirs), custom_call_target="tpu_custom_call" | custom-call | flops 3221225472 | bytes 524292 | tf_op jit(solution)/shard_map/pallas_call | solution.py:242
  67.8 3.4 %shard_map.61.refs_0_ = f32[864,256]{1,0:T(8,128)S(1)} custom-call(bf16[128,1024]{1,0:T(8,128)(2,1)} %get-tuple-element.24.slopes, bf16[2,256,1024]{2,1,0:T(8,128)(2,1)S(1)} %copy-done.1, f32[864,256]{1,0:T(8,128)S(1)} %shard_map.60.refs_0_), custom_call_target="tpu_custom_call", output_to_operand_aliasing={{}: (2, {})} | custom-call | flops 905969664 | bytes 3080192 | tf_op jit(solution)/shard_map/pallas_call | solution.py:242
  71.9 3.1 %shard_map.55 = (bf16[64,1024]{1,0:T(8,128)(2,1)S(1)}, bf16[64,1024]{1,0:T(8,128)(2,1)S(1)}, bf16[2,256,1024]{2,1,0:T(8,128)(2,1)S(1)}) custom-call(s32[1]{0:T(128)} %bitcast.1.core, bf16[864,256]{1,0:T(8,128)(2,1)S(1)} %shard_map.50.kernel, bf16[128,1024]{1,0:T(8,128)(2,1)} %collective-permute-done.11.refs_0_, ...), custom_call_target="tpu_custom_call" | custom-call | flops 905969664 | bytes 3063812 | tf_op jit(solution)/shard_map/pallas_call | solution.py:242
  76.7 2.4 %shard_map.62.refs_0_ = f32[864,256]{1,0:T(8,128)S(1)} custom-call(bf16[128,1024]{1,0:T(8,128)(2,1)S(1)} %get-tuple-element.27.slopes, bf16[2,256,1024]{2,1,0:T(8,128)(2,1)S(1)} %get-tuple-element.37.inputs, f32[864,256]{1,0:T(8,128)S(1)} %shard_map.61.refs_0_), custom_call_target="tpu_custom_call", output_to_operand_aliasing={{}: (2, {})} | custom-call | flops 905969664 | bytes 3080192 | tf_op jit(solution)/shard_map/pallas_call | solution.py:242
  79.4 2.4 %shard_map.63 = f32[864,256]{1,0:T(8,128)S(1)} custom-call(bf16[64,1024]{1,0:T(8,128)(2,1)S(1)} %get-tuple-element.33.slopes, bf16[2,256,1024]{2,1,0:T(8,128)(2,1)S(1)} %get-tuple-element.36.inputs, f32[864,256]{1,0:T(8,128)S(1)} %shard_map.62.refs_0_), custom_call_target="tpu_custom_call", output_to_operand_aliasing={{}: (2, {})} | custom-call | flops 905969664 | bytes 2949120 | tf_op jit(solution)/shard_map/pallas_call | solution.py:242
  87.5 2.1 %collective-permute-start.41 = (bf16[64,864]{1,0:T(8,128)(2,1)S(1)}, bf16[64,864]{1,0:T(8,128)(2,1)S(1)}, u32[]{:S(2)}, u32[]{:S(2)}) collective-permute-start(bf16[64,864]{1,0:T(8,128)(2,1)S(1)} %get-tuple-element.53), channel_id=1, source_target_pairs={{0,2},{1,3},{2,0},{3,1},{4,6},{5,7},{6,4},{7,5},{8,10},{9,11},{10,... | collective-permute-start | bytes 331784 | tf_op jit(solution)/shard_map/ppermute | solution.py:31
  89.6 2.5 %collective-permute-start.43 = (bf16[64,864]{1,0:T(8,128)(2,1)S(1)}, bf16[64,864]{1,0:T(8,128)(2,1)S(1)}, u32[]{:S(2)}, u32[]{:S(2)}) collective-permute-start(bf16[64,864]{1,0:T(8,128)(2,1)S(1)} %get-tuple-element.54), channel_id=1, source_target_pairs={{0,6},{1,7},{2,4},{3,5},{4,2},{5,3},{6,0},{7,1},{8,14},{9,15},{10,... | collective-permute-start | bytes 331784 | tf_op jit(solution)/shard_map/ppermute | solution.py:31
  98.6 4.8 %collective-permute-done.42 = bf16[64,864]{1,0:T(8,128)(2,1)S(1)} collective-permute-done((bf16[64,864]{1,0:T(8,128)(2,1)S(1)}, bf16[64,864]{1,0:T(8,128)(2,1)S(1)}, u32[]{:S(2)}, u32[]{:S(2)}) %collective-permute-start.42) | collective-permute-done | bytes 110624 | tf_op jit(solution)/shard_map/ppermute | solution.py:31
  114.8 4.0 %shard_map.58.inverse = f32[256,256]{1,0:T(8,128)S(1)} custom-call(s32[1]{0:T(128)} %bitcast.1.core, f32[128,256]{1,0:T(8,128)S(1)} %constant_dynamic-update-slice_fusion.mine, f32[128,256]{1,0:T(8,128)S(1)} %collective-permute-done.36.theirs), custom_call_target="tpu_custom_call" | custom-call | flops 3221225472 | bytes 524292 | tf_op jit(solution)/shard_map/pallas_call | solution.py:242
  120.6 4.5 %collective-permute-done.46.refs_2_ = f32[64,864]{1,0:T(8,128)S(1)} collective-permute-done((f32[64,864]{1,0:T(8,128)S(1)}, f32[64,864]{1,0:T(8,128)S(1)}, u32[]{:S(2)}, u32[]{:S(2)}) %collective-permute-start.46) | collective-permute-done | bytes 221216 | tf_op jit(solution)/shard_map/ppermute | solution.py:31
  125.1 2.0 %shard_map.64 = f32[864,256]{1,0:T(8,128)} custom-call(s32[1]{0:T(128)} %bitcast.at, f32[256,256]{1,0:T(8,128)S(1)} %shard_map.58.inverse, f32[64,864]{1,0:T(8,128)S(1)} %maximum_select_fusion.refs_0_, f32[64,864]{1,0:T(8,128)S(1)} %collective-permute-done.45.refs_1_, f32[64,864]{1,0:T(8,128)S(1)} %collective-permute-done.46.refs_2_, ...), custom_call_target="tpu_custom_call" | custom-call | flops 679477248 | bytes 2031620 | tf_op jit(solution)/shard_map/pallas_call | solution.py:242
  (126 shorter events, 53.3 us)
Async XLA Ops:
  3.9 24.1 %collective-permute-start.6 = (bf16[320,1024]{1,0:T(8,128)(2,1)}, bf16[320,1024]{1,0:T(8,128)(2,1)S(1)}, u32[]{:S(2)}, u32[]{:S(2)}) collective-permute-start(bf16[320,1024]{1,0:T(8,128)(2,1)} %get-tuple-element.50), channel_id=1, source_target_pairs={{0,16},{1,17},{2,18},{3,19},{4,20},{5,21},{6,22},{7,23},{8,24},{9,... | collective-permute-start | bytes 1966088 | tf_op jit(solution)/shard_map/ppermute | solution.py:31
  6.9 21.2 %collective-permute-start.5 = (bf16[320,1024]{1,0:T(8,128)(2,1)}, bf16[320,1024]{1,0:T(8,128)(2,1)S(1)}, u32[]{:S(2)}, u32[]{:S(2)}) collective-permute-start(bf16[320,1024]{1,0:T(8,128)(2,1)} %get-tuple-element.51), channel_id=1, source_target_pairs={{0,8},{1,9},{2,10},{3,11},{4,12},{5,13},{6,14},{7,15},{8,0},{9,1},... | collective-permute-start | bytes 1966088 | tf_op jit(solution)/shard_map/ppermute | solution.py:31
  8.4 19.7 %collective-permute-start.4 = (bf16[320,1024]{1,0:T(8,128)(2,1)S(1)}, bf16[320,1024]{1,0:T(8,128)(2,1)S(1)}, u32[]{:S(2)}, u32[]{:S(2)}) collective-permute-start(bf16[320,1024]{1,0:T(8,128)(2,1)S(1)} %get-tuple-element.52.refs_0_.mine), channel_id=1, source_target_pairs={{0,1},{1,0},{2,3},{3,2},{4,5},{5,4},{6,7},{7,6},{8,9},{9,8},{10,11... | collective-permute-start | bytes 1966088 | tf_op jit(solution)/shard_map/ppermute | solution.py:31
  15.1 10.3 %collective-permute-start.2 = (bf16[64,864]{1,0:T(8,128)(2,1)S(1)}, bf16[64,864]{1,0:T(8,128)(2,1)S(1)}, u32[]{:S(2)}, u32[]{:S(2)}) collective-permute-start(bf16[64,864]{1,0:T(8,128)(2,1)S(1)} %maximum_select_fusion.1.refs_0_), channel_id=1, source_target_pairs={{0,4},{1,5},{2,6},{3,7},{4,0},{5,1},{6,2},{7,3},{8,12},{9,13},{10,... | collective-permute-start | bytes 331784 | tf_op jit(solution)/shard_map/ppermute | solution.py:31
  31.7 9.5 %collective-permute-start.14 = (f32[128,256]{1,0:T(8,128)S(1)}, f32[128,256]{1,0:T(8,128)S(1)}, u32[]{:S(2)}, u32[]{:S(2)}) collective-permute-start(f32[128,256]{1,0:T(8,128)S(1)} %shard_map.54), channel_id=1, source_target_pairs={{0,6},{1,7},{2,4},{3,5},{4,2},{5,3},{6,0},{7,1},{8,14},{9,15},{10,... | collective-permute-start | bytes 393224 | tf_op jit(solution)/shard_map/ppermute | solution.py:31
  33.3 13.2 %collective-permute-start.13 = (f32[128,256]{1,0:T(8,128)S(1)}, f32[128,256]{1,0:T(8,128)S(1)}, u32[]{:S(2)}, u32[]{:S(2)}) collective-permute-start(f32[128,256]{1,0:T(8,128)S(1)} %shard_map.54), channel_id=1, source_target_pairs={{0,4},{1,5},{2,6},{3,7},{4,0},{5,1},{6,2},{7,3},{8,12},{9,13},{10,... | collective-permute-start | bytes 393224 | tf_op jit(solution)/shard_map/ppermute | solution.py:31
  34.2 12.3 %collective-permute-start.12 = (f32[128,256]{1,0:T(8,128)S(1)}, f32[128,256]{1,0:T(8,128)S(1)}, u32[]{:S(2)}, u32[]{:S(2)}) collective-permute-start(f32[128,256]{1,0:T(8,128)S(1)} %shard_map.54), channel_id=1, source_target_pairs={{0,2},{1,3},{2,0},{3,1},{4,6},{5,7},{6,4},{7,5},{8,10},{9,11},{10,... | collective-permute-start | bytes 393224 | tf_op jit(solution)/shard_map/ppermute | solution.py:31
  36.2 10.9 %collective-permute-start.15 = (bf16[128,1024]{1,0:T(8,128)(2,1)S(1)}, bf16[128,1024]{1,0:T(8,128)(2,1)S(1)}, u32[]{:S(2)}, u32[]{:S(2)}) collective-permute-start(bf16[128,1024]{1,0:T(8,128)(2,1)S(1)} %slice.7), channel_id=1, source_target_pairs={{0,8},{1,9},{2,10},{3,11},{4,12},{5,13},{6,14},{7,15},{8,0},{9,1},... | collective-permute-start | bytes 786440 | tf_op jit(solution)/shard_map/ppermute | solution.py:31
  36.8 10.5 %collective-permute-start.11 = (bf16[128,1024]{1,0:T(8,128)(2,1)S(1)}, bf16[128,1024]{1,0:T(8,128)(2,1)}, u32[]{:S(2)}, u32[]{:S(2)}) collective-permute-start(bf16[128,1024]{1,0:T(8,128)(2,1)S(1)} %slice.6), channel_id=1, source_target_pairs={{0,16},{1,17},{2,18},{3,19},{4,20},{5,21},{6,22},{7,23},{8,24},{9,... | collective-permute-start | bytes 786440 | tf_op jit(solution)/shard_map/ppermute | solution.py:31
  46.5 13.9 %collective-permute-start.9 = (bf16[320,1024]{1,0:T(8,128)(2,1)S(1)}, bf16[320,1024]{1,0:T(8,128)(2,1)S(1)}, u32[]{:S(2)}, u32[]{:S(2)}) collective-permute-start(bf16[320,1024]{1,0:T(8,128)(2,1)S(1)} %collective-permute-done.6.refs_0_), channel_id=1, source_target_pairs={{0,1},{1,0},{2,3},{3,2},{4,5},{5,4},{6,7},{7,6},{8,9},{9,8},{10,11... | collective-permute-start | bytes 1966088 | tf_op jit(solution)/shard_map/ppermute | solution.py:31
  59.0 12.2 %collective-permute-start.8 = (bf16[128,1024]{1,0:T(8,128)(2,1)}, bf16[128,1024]{1,0:T(8,128)(2,1)S(1)}, u32[]{:S(2)}, u32[]{:S(2)}) collective-permute-start(bf16[128,1024]{1,0:T(8,128)(2,1)} %get-tuple-element.24.slopes), channel_id=1, source_target_pairs={{0,8},{1,9},{2,10},{3,11},{4,12},{5,13},{6,14},{7,15},{8,0},{9,1},... | collective-permute-start | bytes 786440 | tf_op jit(solution)/shard_map/ppermute | solution.py:31
  62.6 16.6 %collective-permute-start.10 = (bf16[128,1024]{1,0:T(8,128)(2,1)S(1)}, bf16[128,1024]{1,0:T(8,128)(2,1)S(1)}, u32[]{:S(2)}, u32[]{:S(2)}) collective-permute-start(bf16[128,1024]{1,0:T(8,128)(2,1)S(1)} %get-tuple-element.27.slopes), channel_id=1, source_target_pairs={{0,16},{1,17},{2,18},{3,19},{4,20},{5,21},{6,22},{7,23},{8,24},{9,... | collective-permute-start | bytes 786440 | tf_op jit(solution)/shard_map/ppermute | solution.py:31
  63.1 8.6 %collective-permute-start.19 = (bf16[64,1024]{1,0:T(8,128)(2,1)S(1)}, bf16[64,1024]{1,0:T(8,128)(2,1)S(1)}, u32[]{:S(2)}, u32[]{:S(2)}) collective-permute-start(bf16[64,1024]{1,0:T(8,128)(2,1)S(1)} %collective-permute-done.16.refs_2_), channel_id=1, source_target_pairs={{0,1},{1,0},{2,3},{3,2},{4,5},{5,4},{6,7},{7,6},{8,9},{9,8},{10,11... | collective-permute-start | bytes 393224 | tf_op jit(solution)/shard_map/ppermute | solution.py:31
  63.1 8.7 %collective-permute-start.17 = (bf16[128,1024]{1,0:T(8,128)(2,1)}, bf16[128,1024]{1,0:T(8,128)(2,1)S(1)}, u32[]{:S(2)}, u32[]{:S(2)}) collective-permute-start(bf16[128,1024]{1,0:T(8,128)(2,1)} %collective-permute-done.11.refs_0_), channel_id=1, source_target_pairs={{0,1},{1,0},{2,3},{3,2},{4,5},{5,4},{6,7},{7,6},{8,9},{9,8},{10,11... | collective-permute-start | bytes 786440 | tf_op jit(solution)/shard_map/ppermute | solution.py:31
  71.2 12.1 %collective-permute-start.21 = (bf16[128,1024]{1,0:T(8,128)(2,1)S(1)}, bf16[128,1024]{1,0:T(8,128)(2,1)S(1)}, u32[]{:S(2)}, u32[]{:S(2)}) collective-permute-start(bf16[128,1024]{1,0:T(8,128)(2,1)S(1)} %get-tuple-element.21.refs_0_.slopes), channel_id=1, source_target_pairs={{0,1},{1,0},{2,3},{3,2},{4,5},{5,4},{6,7},{7,6},{8,9},{9,8},{10,11... | collective-permute-start | bytes 786440 | tf_op jit(solution)/shard_map/ppermute | solution.py:31
  71.8 11.5 %collective-permute-start.22 = (bf16[128,1024]{1,0:T(8,128)(2,1)S(1)}, bf16[128,1024]{1,0:T(8,128)(2,1)S(1)}, u32[]{:S(2)}, u32[]{:S(2)}) collective-permute-start(bf16[128,1024]{1,0:T(8,128)(2,1)S(1)} %collective-permute-done.8.refs_1_), channel_id=1, source_target_pairs={{0,1},{1,0},{2,3},{3,2},{4,5},{5,4},{6,7},{7,6},{8,9},{9,8},{10,11... | collective-permute-start | bytes 786440 | tf_op jit(solution)/shard_map/ppermute | solution.py:31
  89.6 9.0 %collective-permute-start.43 = (bf16[64,864]{1,0:T(8,128)(2,1)S(1)}, bf16[64,864]{1,0:T(8,128)(2,1)S(1)}, u32[]{:S(2)}, u32[]{:S(2)}) collective-permute-start(bf16[64,864]{1,0:T(8,128)(2,1)S(1)} %get-tuple-element.54), channel_id=1, source_target_pairs={{0,6},{1,7},{2,4},{3,5},{4,2},{5,3},{6,0},{7,1},{8,14},{9,15},{10,... | collective-permute-start | bytes 331784 | tf_op jit(solution)/shard_map/ppermute | solution.py:31
  92.1 11.3 %collective-permute-start.42 = (bf16[64,864]{1,0:T(8,128)(2,1)S(1)}, bf16[64,864]{1,0:T(8,128)(2,1)S(1)}, u32[]{:S(2)}, u32[]{:S(2)}) collective-permute-start(bf16[64,864]{1,0:T(8,128)(2,1)S(1)} %get-tuple-element.55), channel_id=1, source_target_pairs={{0,4},{1,5},{2,6},{3,7},{4,0},{5,1},{6,2},{7,3},{8,12},{9,13},{10,... | collective-permute-start | bytes 331784 | tf_op jit(solution)/shard_map/ppermute | solution.py:31
  92.1 11.3 %collective-permute-start.30 = (f32[32,256]{1,0:T(8,128)S(1)}, f32[32,256]{1,0:T(8,128)S(1)}, u32[]{:S(2)}, u32[]{:S(2)}) collective-permute-start(f32[32,256]{1,0:T(8,128)S(1)} %add_add_fusion.3), channel_id=1, source_target_pairs={{0,6},{1,7},{2,4},{3,5},{4,2},{5,3},{6,0},{7,1},{8,14},{9,15},{10,... | collective-permute-start | bytes 98312 | tf_op jit(solution)/shard_map/ppermute | solution.py:31
  93.9 10.2 %collective-permute-start.29 = (f32[32,256]{1,0:T(8,128)S(1)}, f32[32,256]{1,0:T(8,128)S(1)}, u32[]{:S(2)}, u32[]{:S(2)}) collective-permute-start(f32[32,256]{1,0:T(8,128)S(1)} %add_add_fusion.3), channel_id=1, source_target_pairs={{0,4},{1,5},{2,6},{3,7},{4,0},{5,1},{6,2},{7,3},{8,12},{9,13},{10,... | collective-permute-start | bytes 98312 | tf_op jit(solution)/shard_map/ppermute | solution.py:31
  111.2 9.4 %collective-permute-start.47 = (f32[64,864]{1,0:T(8,128)S(1)}, f32[64,864]{1,0:T(8,128)S(1)}, u32[]{:S(2)}, u32[]{:S(2)}) collective-permute-start(f32[64,864]{1,0:T(8,128)S(1)} %maximum_select_fusion.refs_0_), channel_id=1, source_target_pairs={{0,24},{1,25},{2,26},{3,27},{4,28},{5,29},{6,30},{7,31},{8,16},{9,... | collective-permute-start | bytes 663560 | tf_op jit(solution)/shard_map/ppermute | solution.py:31
  112.8 12.3 %collective-permute-start.46 = (f32[64,864]{1,0:T(8,128)S(1)}, f32[64,864]{1,0:T(8,128)S(1)}, u32[]{:S(2)}, u32[]{:S(2)}) collective-permute-start(f32[64,864]{1,0:T(8,128)S(1)} %maximum_select_fusion.refs_0_), channel_id=1, source_target_pairs={{0,16},{1,17},{2,18},{3,19},{4,20},{5,21},{6,22},{7,23},{8,24},{9,... | collective-permute-start | bytes 663560 | tf_op jit(solution)/shard_map/ppermute | solution.py:31
  114.1 11.0 %collective-permute-start.45 = (f32[64,864]{1,0:T(8,128)S(1)}, f32[64,864]{1,0:T(8,128)S(1)}, u32[]{:S(2)}, u32[]{:S(2)}) collective-permute-start(f32[64,864]{1,0:T(8,128)S(1)} %maximum_select_fusion.refs_0_), channel_id=1, source_target_pairs={{0,8},{1,9},{2,10},{3,11},{4,12},{5,13},{6,14},{7,15},{8,0},{9,1},... | collective-permute-start | bytes 663560 | tf_op jit(solution)/shard_map/ppermute | solution.py:31
  114.8 12.3 %collective-permute-start.32 = (bf16[64,1024]{1,0:T(8,128)(2,1)S(1)}, bf16[64,1024]{1,0:T(8,128)(2,1)S(1)}, u32[]{:S(2)}, u32[]{:S(2)}) collective-permute-start(bf16[64,1024]{1,0:T(8,128)(2,1)S(1)} %collective-permute-done.31.refs_3_), channel_id=1, source_target_pairs={{0,1},{1,0},{2,3},{3,2},{4,5},{5,4},{6,7},{7,6},{8,9},{9,8},{10,11... | collective-permute-start | bytes 393224 | tf_op jit(solution)/shard_map/ppermute | solution.py:31
  (31 other events, 164.0 us)
where the time goes:
time: 128 us
  starting transfers between devices  51.9 us (41%)
  Pallas kernels  32.7 us (26%)
  waiting for transfers between devices  32.5 us (25%)
  local copies, waits for them, and re-layouts  7.11 us (6%)
  other arithmetic  1.56 us (1%)
    ppermute x48, starting transfers between devices, exchange(): return lax.ppermute(x, AXES, perm)  51.9 us
    pallas_call x15, Pallas kernels, call(): pl.pallas_call(kernel, out_shape=tuple(shapes), in_specs=[SMEM] * scalars...  32.7 us
    ppermute x48, waiting for transfers between devices, exchange(): return lax.ppermute(x, AXES, perm)  32.5 us
    unnamed x14, local copies, waits for them, and re-layouts  3.25 us
  transfers between devices with their start and end apart: 48, of which 16 were waited for; matrix products, arithmetic and copies ran while one was open for 3% of the time, Pallas kernels for 23%

commit v1 on v0

v1 whole, which is shorter than its diff:
```python
import functools
import math

import jax
import jax.numpy as jnp
import numpy as np
from jax import lax
from jax.experimental import pallas as pl
from jax.experimental.pallas import tpu as pltpu
from jax.sharding import PartitionSpec as P

SX = 4
SY = 16
SZ = 16
NS_ITERS = 8
DAMPING = 0.001
AXES = ("dp", "shard")
NT = (((1,), (1,)), ((), ()))
VMEM = pl.BlockSpec(memory_space=pltpu.VMEM)
ANY = pl.BlockSpec(memory_space=pl.ANY)
HBM = pl.BlockSpec(memory_space=pltpu.HBM)
SMEM = pl.BlockSpec(memory_space=pltpu.SMEM)
PARAMS = pltpu.CompilerParams(vmem_limit_bytes=32 * 1024 * 1024)


def exchange(x, planes, pairs, dp=0, z=0, core=0):
    perm = []
    for a in range(planes):
        for b in range(pairs):
            for c in range(2):
                here = (a * pairs + b) * 2 + c
                there = ((a ^ dp) * pairs + (b ^ z)) * 2 + (c ^ core)
                perm.append((here, there))
    return lax.ppermute(x, AXES, perm)


def after(x, *others):
    return lax.optimization_barrier((x, *others))[0]


def rows_of(x, index, height):
    return lax.dynamic_slice_in_dim(x, index * height, height, 0)


def place(buffer, block, index):
    return lax.dynamic_update_slice_in_dim(buffer, block, index * block.shape[0], 0)


def by_core(core, mine, other):
    return jnp.where(
        core == 0, jnp.concatenate([mine, other]), jnp.concatenate([other, mine])
    )


def dot3(left, right, dims=(((1,), (0,)), ((), ()))):
    left_high = left.astype(jnp.bfloat16)
    left_low = (left - left_high.astype(jnp.float32)).astype(jnp.bfloat16)
    right_high = right.astype(jnp.bfloat16)
    right_low = (right - right_high.astype(jnp.float32)).astype(jnp.bfloat16)

    def dot(a, b):
        return lax.dot_general(a, b, dims, preferred_element_type=jnp.float32)

    return dot(left_high, right_high) + (dot(left_high, right_low) + dot(left_low, right_high))


def shift_matrices():
    cell = np.arange(SY * SZ)
    parts = []
    for b in range(3):
        for c in range(3):
            meets_y = cell[:, None] // SZ + (b - 1) == cell[None, :] // SZ
            meets_z = cell[:, None] % SZ + (c - 1) == cell[None, :] % SZ
            parts.append(meets_y & meets_z)
    return jnp.asarray(np.concatenate(parts, axis=1), jnp.bfloat16)


def columns_kernel(pairs, out, at, *refs):
    blocks, (result, rows) = refs[:pairs], refs[pairs:]
    height = blocks[0].shape[0]
    channels = rows.shape[0]
    for step in range(pairs):
        start = pl.multiple_of((at[0] ^ step) * height, height)
        rows[pl.ds(start, height), :] = blocks[step][...].astype(jnp.float32)
    turned = rows[...].T.astype(jnp.bfloat16)
    for over in range(9):
        for c in range(3):
            tap = 3 * over + c
            result[over * out : (over + 1) * out, c * channels : (c + 1) * channels] = turned[
                tap * out : (tap + 1) * out, :
            ]


def slab(index):
    return slice(index * SY * SZ, (index + 1) * SY * SZ)


def forward_window(out, kernel, shifts, cot, stack, wide):
    channels, cells = stack.shape[0] // 3, stack.shape[1]
    for index in range(SX):
        middle = stack[channels : 2 * channels, slab(index)]
        for c, offset in ((0, 1), (2, 0)):
            stack[c * channels : (c + 1) * channels, slab(index)] = jnp.dot(
                middle, shifts[:, slab(offset)], preferred_element_type=jnp.float32
            ).astype(jnp.bfloat16)
    wide[...] = jnp.dot(kernel[...], stack[...], preferred_element_type=jnp.float32)
    along_y = lax.broadcasted_iota(jnp.int32, (out, cells), 1) // SZ % SY
    edge = jnp.zeros((out, SY * SZ), jnp.float32)
    outputs = None
    for a in range(3):
        first = 3 * a * out
        below = pltpu.roll(wide[first : first + out, :], SZ, 1)
        above = pltpu.roll(wide[first + 2 * out : first + 3 * out, :], cells - SZ, 1)
        part = (
            wide[first + out : first + 2 * out, :]
            + jnp.where(along_y > 0, below, 0.0)
            + jnp.where(along_y < SY - 1, above, 0.0)
        )
        if a == 0:
            part = jnp.concatenate([edge, part[:, : cells - SY * SZ]], axis=1)
        elif a == 2:
            part = jnp.concatenate([part[:, SY * SZ :], edge], axis=1)
        outputs = part if outputs is None else outputs + part
    sigma = jax.nn.sigmoid(outputs)
    activated = (outputs * sigma).astype(jnp.bfloat16)
    slope = cot.astype(jnp.float32) * sigma * (1.0 + outputs * (1.0 - sigma))
    return activated, slope.astype(jnp.bfloat16)


def gradient_windows(out, shifts, slopes, inputs, total_in, total, rows, moved):
    for window in range(2):
        for index in range(SX):
            start = (window * SX + index) * out
            rows[start : start + out, :] = slopes[
                window * out : (window + 1) * out, slab(index)
            ]
    for over in range(9):
        shifted = jnp.dot(
            rows[...], shifts[:, slab(over)], preferred_element_type=jnp.float32
        ).astype(jnp.bfloat16)
        for window in range(2):
            for index in range(SX):
                start = (window * SX + index) * out
                moved[window, over * out : (over + 1) * out, slab(index)] = shifted[
                    start : start + out, :
                ]
    height = 9 * out
    cells = moved.shape[2]
    near, far = slice(0, cells - SY * SZ), slice(SY * SZ, cells)
    spans = ((far, near), (slice(0, cells), slice(0, cells)), (near, far))
    for a, (of_slope, of_input) in enumerate(spans):
        sums = None
        for window in range(2):
            part = lax.dot_general(
                moved[window, :, of_slope],
                inputs[window][:, of_input],
                NT,
                preferred_element_type=jnp.float32,
            )
            sums = part if sums is None else sums + part
        at = slice(a * height, (a + 1) * height)
        total[at, :] = sums if total_in is None else total_in[at, :] + sums


def load(copies, semaphores):
    started = [
        pltpu.make_async_copy(source, target, semaphores.at[index])
        for index, (source, target) in enumerate(copies)
    ]
    for copy in started:
        copy.start()
    return started


def window_copies(pieces, inputs):
    copies = []
    start = 0
    for piece, height in pieces:
        copies.append((piece.at[pl.ds(0, height)], inputs.at[pl.ds(start, height)]))
        start += height
    return copies


def split(refs, heights):
    chips = []
    for parts in heights:
        count = len(parts)
        chips.append(
            (tuple(zip(refs[:count], parts)), tuple(zip(refs[count : 2 * count], parts)))
        )
        refs = refs[2 * count :]
    return chips, refs


def gather_window(pieces, inputs):
    start = 0
    for piece, height in pieces:
        inputs[start : start + height, :] = piece[:height, :]
        start += height


def forward_chip(out, core, kernel, for_z, windows, slopes, acts, stack, wide, gram):
    channels = stack.shape[0] // 3
    inputs = stack.at[channels : 2 * channels]
    half = channels // 2
    own = pl.multiple_of(core[0] * half, half)
    for window, pieces in enumerate(windows):
        gather_window(pieces, inputs)
        piece, height = pieces[0]
        first = pl.multiple_of(height + core[0] * out, out)
        at = slice(window * out, (window + 1) * out)
        acts[at, :], slopes[at, :] = forward_window(
            out, kernel, for_z, piece[pl.ds(first, out), :], stack, wide
        )
        part = lax.dot_general(
            inputs[pl.ds(own, half), :], inputs[...], NT, preferred_element_type=jnp.float32
        )
        gram = part if gram is None else gram + part
    return gram


def first_kernel(out, core, kernel, for_z, shifts, mine, theirs, *refs):
    stack, wide, held, semaphores, matrices, rows, moved = refs[-7:]
    refs = refs[:-7]
    chips = (len(refs) - 3) // 3
    payloads, (gram, total, *results) = refs[: 2 * chips], refs[2 * chips :]
    started = load(
        [(shifts, matrices), (mine, held.at[0]), (theirs, held.at[1])], semaphores
    )
    channels = gram.shape[1]
    sums = None
    windows = [payloads[2 * chip : 2 * chip + 2] for chip in range(chips)]
    for chip, pair in enumerate(windows + [(held.at[0], held.at[1])]):
        if chip == chips:
            for copy in started[1:]:
                copy.wait()
        result = results[(chip + 1) % (chips + 1)]
        pieces = tuple(((payload, channels),) for payload in pair)
        slopes, acts = result.at[: 2 * out], result.at[2 * out :]
        sums = forward_chip(out, core, kernel, for_z, pieces, slopes, acts, stack, wide, sums)
        if chip == 0:
            started[0].wait()
        inputs = tuple(payload.at[:channels] for payload in pair)
        gradient_windows(
            out, matrices, slopes, inputs, None if chip == 0 else total, total, rows, moved
        )
    gram[...] = sums


def last_kernel(out, heights, core, kernel, for_z, *refs):
    (windows,), (gram_in, gram, result, stack, wide) = split(refs, [heights])
    slopes, acts = result.at[: 2 * out], result.at[2 * out :]
    gram[...] = forward_chip(
        out, core, kernel, for_z, windows, slopes, acts, stack, wide, gram_in[...]
    )


def gradient_kernel(out, heights, shifts, slopes, total_in, *refs):
    (windows,), (total, inputs, rows, moved) = split(refs, [heights])
    for window, pieces in enumerate(windows):
        gather_window(pieces, inputs.at[window])
    gradient_windows(
        out, shifts, slopes, (inputs.at[0], inputs.at[1]), total_in, total, rows, moved
    )


def payload_kernel(planes, out, at, inputs, cotangent, *refs):
    payloads, (held, semaphores) = refs[:-2], refs[-2:]
    channels = inputs.shape[0]
    half = channels // 2
    for copy in load([(inputs, held.at[0]), (cotangent, held.at[1])], semaphores):
        copy.wait()
    for payload, steps in zip(payloads, payload_steps(planes)):
        payload[:channels, :] = held[0]
        start = channels
        for step in steps:
            for core in range(2):
                first = pl.multiple_of(core * half + (at[0] ^ step) * out, out)
                payload[start : start + out, :] = held[1, pl.ds(first, out), :]
                start += out


def payload_steps(planes):
    if planes == 4:
        return [(0,), (1, 3), (2,)]
    return [(step,) for step in range(planes)]


def halves_kernel(channels, split_at, first, second, low, high):
    low[:split_at, :] = first[:split_at, :]
    low[split_at:, :] = first[channels + low.shape[0] - split_at :, :]
    high[...] = second[split_at:channels, :]


def gram_kernel(planes, out, at, core, *refs):
    mine, theirs = refs[:planes], refs[planes : 2 * planes]
    result, slopes, semaphores = refs[2 * planes :]
    half = result.shape[0]
    cells = mine[0].shape[1]
    own = pl.multiple_of(core[0] * half, half)
    other = pl.multiple_of((1 - core[0]) * half, half)
    copies = []
    for step in range(planes):
        plane = (at[0] ^ step) * out
        for window in range(2):
            columns = pl.ds(window * cells, cells)
            for start, piece, rows in (
                (own, mine[step], window * out),
                (other, theirs[step], (1 - window) * out),
            ):
                target = pl.multiple_of(start + plane, out)
                copies.append(
                    (piece.at[pl.ds(rows, out)], slopes.at[pl.ds(target, out), columns])
                )
    for copy in load(copies, semaphores):
        copy.wait()
    result[...] = lax.dot_general(
        slopes[pl.ds(own, half), :], slopes[...], NT, preferred_element_type=jnp.float32
    )


def product_kernel(pairs, core, inverse, mine, theirs, result, narrow, rows):
    height = inverse.shape[0] // (2 * pairs)
    for pair in range(pairs):
        start = pl.multiple_of((2 * pair + core[0]) * height, height)
        rows[pair * height : (pair + 1) * height, :] = inverse[pl.ds(start, height), :]
    for index, gradient in ((core[0], mine), (1 - core[0], theirs)):
        product = dot3(rows[...], gradient[...], NT)
        result[index] = product
        narrow[index] = product.astype(jnp.bfloat16)


def sort_kernel(planes, out, at, core, *refs):
    mine, theirs = refs[:planes], refs[planes : 2 * planes]
    result, semaphores = refs[2 * planes :]
    half = result.shape[0] // 2
    copies = []
    for step in range(planes):
        plane = (at[0] ^ step) * out
        first = mine[step].shape[0] - 2 * out
        for start, piece, rows in (
            (core[0] * half, mine[step], first),
            ((1 - core[0]) * half, theirs[step], first + out),
        ):
            target = pl.multiple_of(start + plane, out)
            copies.append((piece.at[pl.ds(rows, out)], result.at[pl.ds(target, out)]))
    for copy in load(copies, semaphores):
        copy.wait()


def newton_kernel(count, core, mine, theirs, result, matrix, both):
    half, size = mine.shape
    matrix[pl.ds(pl.multiple_of(core[0] * half, half), half), :] = mine[...]
    matrix[pl.ds(pl.multiple_of((1 - core[0]) * half, half), half), :] = theirs[...]
    row = lax.broadcasted_iota(jnp.int32, (size, size), 0)
    column = lax.broadcasted_iota(jnp.int32, (size, size), 1)
    identity = jnp.where(row == column, 1.0, 0.0)
    factor = matrix[...] / count + DAMPING * identity
    diagonal = jnp.sum(factor * identity, axis=1, keepdims=True)
    scale = 1.0 / jnp.sum(diagonal, axis=0, keepdims=True)
    error = identity - factor * scale
    both[:size, :] = (identity + error) * scale
    both[size:, :] = error
    for sweep in range(1, NS_ITERS):
        if sweep == 1:
            both[size:, :] = dot3(error, error)
        last = sweep == NS_ITERS - 1
        products = dot3(both[:size, :] if last else both[...], both[size:, :])
        both[:size, :] += products[:size]
        if not last:
            both[size:, :] = products[size:]
    result[...] = both[:size, :]


def update_kernel(planes, taps, out, scale, at, inverse, *refs):
    pieces, (result, rows, factor) = refs[:planes], refs[planes:]
    own_rows = pieces[0].shape[1]
    half = inverse.shape[0] // 2
    for step in range(planes):
        for core in range(2):
            block = (step * 2 + core) * out
            start = pl.multiple_of(core * half + (at[0] ^ step) * out, out)
            factor[block : block + out, :] = inverse[pl.ds(start, out), :]
            for tap in range(taps):
                rows[tap * own_rows : (tap + 1) * own_rows, block : block + out] = pieces[step][
                    core, :, tap * out : (tap + 1) * out
                ]
    result[...] = dot3(rows[...], factor[...]) * scale


def call(kernel, args, shapes, scratch, flops, scalars=0, aliases=None, far=(), spec=ANY):
    moved = sum(a.size * a.dtype.itemsize for a in list(args) + list(shapes))
    in_specs = [SMEM] * scalars + [VMEM] * (len(args) - scalars)
    for index in far:
        in_specs[index] = spec
    return pl.pallas_call(
        kernel,
        out_shape=tuple(shapes),
        in_specs=in_specs,
        out_specs=tuple([VMEM] * len(shapes)),
        scratch_shapes=scratch,
        input_output_aliases=aliases or {},
        compiler_params=PARAMS,
        cost_estimate=pl.CostEstimate(flops=flops, bytes_accessed=moved, transcendentals=0),
    )(*args)


def shards(planes, pairs, activations, out_grad, weights):
    f32, bf16 = jnp.float32, jnp.bfloat16
    shape = jax.ShapeDtypeStruct
    inputs = activations[0]
    cotangent = out_grad[0]
    channels, cells = inputs.shape
    own_rows, taps, _ = weights.shape
    out = channels // (2 * planes)
    half = channels // 2
    wide = taps * out
    my_plane = lax.axis_index("dp")
    my_index = lax.axis_index("shard")
    my_pair = my_index // 2
    my_core = my_index % 2
    at_plane = my_plane.reshape(1)
    at_pair = my_pair.reshape(1)
    at_core = my_core.reshape(1)
    swap = functools.partial(exchange, planes=planes, pairs=pairs)

    def kernel_columns(core):
        start = core * half + my_plane * out
        part = lax.dynamic_slice_in_dim(weights, start, out, 2)
        return part.reshape(own_rows, wide)

    block = by_core(my_core, kernel_columns(my_core), swap(kernel_columns(1 - my_core), core=1))
    blocks = [block] + [swap(block, z=step) for step in range(1, pairs)]
    (kernel,) = call(
        functools.partial(columns_kernel, pairs, out),
        (at_pair, *blocks),
        [shape((9 * out, 3 * channels), bf16)],
        [pltpu.VMEM((channels, wide), f32)],
        0,
        scalars=1,
    )

    steps = payload_steps(planes)
    payloads = call(
        functools.partial(payload_kernel, planes, out),
        (at_plane, inputs, cotangent),
        [shape((channels + 2 * out * len(targets), cells), bf16) for targets in steps],
        [pltpu.VMEM((2, channels, cells), bf16), pltpu.SemaphoreType.DMA((2,))],
        0,
        scalars=1,
        far=(1, 2),
        spec=HBM,
    )
    own, *arrived = payloads[:1] + tuple(
        swap(payload, dp=step) for step, payload in enumerate(payloads) if step > 0
    )
    own, *arrived = lax.optimization_barrier((own, *arrived, *blocks))[: len(arrived) + 1]
    windows = [[own]] + [[part] for part in arrived]
    heights = [(channels,)] * len(windows)
    if len(windows) < planes:
        split_at = half - out
        low, high = call(
            functools.partial(halves_kernel, channels, split_at),
            arrived,
            [shape((half + out, cells), bf16)] * 2,
            [],
            0,
        )
        windows.append([swap(low, dp=2), swap(high, dp=1)])
        heights.append((split_at, channels - split_at))

    shifts = shift_matrices()
    half_flops = 2 * 2 * wide * channels * cells

    for_forward = [pltpu.VMEM((3 * channels, cells), bf16), pltpu.VMEM((9 * out, cells), f32)]
    for_gradient = [
        pltpu.VMEM((2 * SX * out, SY * SZ), bf16),
        pltpu.VMEM((2, 9 * out, cells), bf16),
    ]

    for_z = jnp.concatenate(
        [shifts[:, 3 * SY * SZ : 4 * SY * SZ], shifts[:, 5 * SY * SZ : 6 * SY * SZ]], axis=1
    )
    near = [part for ((mine,)) in windows[1:-1] for part in (mine, swap(mine, core=1))]
    a_half, total, *results = call(
        functools.partial(first_kernel, out),
        (at_core, kernel, for_z, shifts, own, swap(own, core=1), *near),
        [shape((half, channels), f32), shape((wide, channels), f32)]
        + [shape((4 * out, cells), bf16)] * (planes - 1),
        for_forward
        + [
            pltpu.VMEM((2, *own.shape), bf16),
            pltpu.SemaphoreType.DMA((3,)),
            pltpu.VMEM(shifts.shape, bf16),
        ]
        + for_gradient,
        2 * half_flops * (planes - 1),
        scalars=1,
        far=(3, 4, 5),
    )
    mine = [after(part, results[-1]) for part in windows[-1]]
    pieces = mine + [swap(part, core=1) for part in mine]
    a_half, result = call(
        functools.partial(last_kernel, out, heights[-1]),
        (at_core, kernel, for_z, *pieces, a_half),
        [shape((half, channels), f32), shape((4 * out, cells), bf16)],
        for_forward,
        half_flops,
        scalars=1,
    )
    (total,) = call(
        functools.partial(gradient_kernel, out, heights[-1]),
        (shifts, result, total, *pieces),
        [shape((wide, channels), f32)],
        [pltpu.VMEM((2, channels, cells), bf16)] + for_gradient,
        half_flops,
        aliases={2: 0},
    )
    back = [results[0]] + [
        swap(part, dp=step) for step, part in enumerate(results) if step > 0
    ]
    back = [after(part, result) for part in back] + [swap(result, dp=planes - 1)]
    theirs = [swap(result, core=1) for result in back]

    part = a_half
    for step in range(1, pairs):
        a_half = a_half + swap(part, z=step)
    a_half = after(a_half, total)

    count = planes * pairs * 2 * cells

    def inverse_of(mine):
        return call(
            functools.partial(newton_kernel, count),
            (at_core, mine, swap(mine, core=1)),
            [shape((channels, channels), f32)],
            [pltpu.VMEM((channels, channels), f32), pltpu.VMEM((2 * channels, channels), f32)],
            6 * NS_ITERS * 4 * channels**3,
            scalars=1,
        )[0]

    (g_half,) = call(
        functools.partial(gram_kernel, planes, out),
        (at_plane, at_core, *back, *theirs),
        [shape((half, channels), f32)],
        [pltpu.VMEM((channels, 2 * cells), bf16), pltpu.SemaphoreType.DMA((4 * planes,))],
        2 * 2 * half * channels * cells,
        scalars=2,
        far=range(2, 2 + 2 * planes),
    )
    inv_a = inverse_of(a_half)
    height = pairs * own_rows
    product, narrow = call(
        functools.partial(product_kernel, pairs),
        (at_core, inv_a, total, swap(total, core=1)),
        [shape((2, height, wide), f32), shape((2, height, wide), bf16)],
        [pltpu.VMEM((height, channels), f32)],
        3 * 2 * channels**2 * wide,
        scalars=1,
    )

    def part_for(array, pair):
        return lax.dynamic_slice_in_dim(array, pair * own_rows, own_rows, 1)

    block = part_for(product, my_pair)
    for step in range(1, pairs):
        block = block + swap(part_for(narrow, my_pair ^ step), z=step).astype(f32)
    g_half = after(g_half, a_half)
    part = rows_of(g_half, my_plane, out)
    for step in range(1, planes):
        part = part + swap(rows_of(g_half, my_plane ^ step, out), dp=step)
    part = after(part, inv_a)
    over_z = part
    for step in range(1, pairs):
        over_z = over_z + swap(part, z=step)
    over_z = after(over_z, narrow)
    g_half = jnp.zeros((half, channels), f32)
    for step in range(planes):
        part = over_z if step == 0 else swap(over_z, dp=step)
        g_half = place(g_half, part, my_plane ^ step)

    inv_g = inverse_of(g_half)

    pieces = [block] + [swap(block, dp=step) for step in range(1, planes)]
    (update,) = call(
        functools.partial(update_kernel, planes, taps, out, 1.0 / math.sqrt(count)),
        (at_plane, inv_g, *pieces),
        [shape((taps * own_rows, channels), f32)],
        [pltpu.VMEM((taps * own_rows, channels), f32), pltpu.VMEM((channels, channels), f32)],
        6 * 2 * taps * own_rows * channels**2,
        scalars=1,
    )
    update = update.reshape(taps, own_rows, channels).transpose(1, 0, 2)

    (activated,) = call(
        functools.partial(sort_kernel, planes, out),
        (at_plane, at_core, *back, *theirs),
        [shape((channels, cells), bf16)],
        [pltpu.SemaphoreType.DMA((2 * planes,))],
        0,
        scalars=2,
        far=range(2, 2 + 2 * planes),
    )
    return activated[None], update


def solution(mesh):
    planes = mesh.shape["dp"]
    pairs = mesh.shape["shard"] // 2
    return jax.shard_map(
        functools.partial(shards, planes, pairs),
        mesh=mesh,
        in_specs=(
            P(("dp", "shard"), None, None),
            P(("dp", "shard"), None, None),
            P("shard", None, None),
        ),
        out_specs=(P(("dp", "shard"), None, None), P("shard", None, None)),
        check_vma=False,
    )
```

time: 128 us -> 112 us (0.88)
  starting transfers between devices: 51.9 us -> 42.8 us
  waiting for transfers between devices: 32.5 us -> 30.4 us
  other arithmetic: 1.56 us -> 0.14 us
    ppermute x48 -> x41, starting transfers between devices: 51.9 us -> 42.8 us  [exchange(): return lax.ppermute(x, AXES, perm)]
    ppermute x48 -> x41, waiting for transfers between devices: 32.5 us -> 30.4 us  [exchange(): return lax.ppermute(x, AXES, perm)]
    dynamic_slice x4 -> x1, local copies, waits for them, and re-layouts: 1.9 us -> 0.02 us  [rows_of(): return lax.dynamic_slice_in_dim(x, index * height, height, 0)]
    concatenate x2 -> x0, other arithmetic: 1.35 us -> none  [the longest x1 1.35 us: shards(): jnp.concatenate([inputs, *cotangent_rows(step)])]
    pallas_call x15 -> x12, Pallas kernels: 32.7 us -> 31.6 us  [call(): pl.pallas_call(kernel, out_shape=tuple(shapes), in_specs=in_specs, out_sp...]
    unnamed x14 -> x18, local copies, waits for them, and re-layouts: 3.25 us -> 3.87 us
  transfers between devices with their start and end apart: 48 -> 41, of which waited for: 16 -> 13; matrix products, arithmetic and copies ran while one was open for 3% -> 2% of each run, Pallas kernels for 23% -> 25%
where the time goes in v1:
time: 112 us
  starting transfers between devices  42.8 us (38%)
  Pallas kernels  31.6 us (28%)
  waiting for transfers between devices  30.4 us (27%)
  local copies, waits for them, and re-layouts  5.86 us (5%)
    ppermute x41, starting transfers between devices, exchange(): return lax.ppermute(x, AXES, perm)  42.8 us
    pallas_call x12, Pallas kernels, call(): pl.pallas_call(kernel, out_shape=tuple(shapes), in_specs=in_specs, out_sp...  31.6 us
    ppermute x41, waiting for transfers between devices, exchange(): return lax.ppermute(x, AXES, perm)  30.4 us
    unnamed x18, local copies, waits for them, and re-layouts  3.87 us
  transfers between devices with their start and end apart: 41, of which 13 were waited for; matrix products, arithmetic and copies ran while one was open for 2% of the time, Pallas kernels for 25%

profile of v1, /device:TPU:0, one launch (start us, length us, event | category | flops | bytes accessed | tf_op | source)
XLA Modules:
  0.0 111.8 jit_solution(1058034772695043744)
XLA Ops:
  3.7 3.0 %collective-permute-start.4 = (bf16[384,1024]{1,0:T(8,128)(2,1)S(1)}, bf16[384,1024]{1,0:T(8,128)(2,1)S(1)}, u32[]{:S(2)}, u32[]{:S(2)}) collective-permute-start(bf16[384,1024]{1,0:T(8,128)(2,1)S(1)} %get-tuple-element.29), channel_id=1, source_target_pairs={{0,8},{1,9},{2,10},{3,11},{4,12},{5,13},{6,14},{7,15},{8,0},{9,1},... | collective-permute-start | bytes 2359304 | tf_op jit(solution)/shard_map/ppermute | solution.py:34
  11.2 1.6 %collective-permute-start.1 = (bf16[64,864]{1,0:T(8,128)(2,1)S(1)}, bf16[64,864]{1,0:T(8,128)(2,1)S(1)}, u32[]{:S(2)}, u32[]{:S(2)}) collective-permute-start(bf16[64,864]{1,0:T(8,128)(2,1)S(1)} %maximum_select_fusion.refs_0_), channel_id=1, source_target_pairs={{0,2},{1,3},{2,0},{3,1},{4,6},{5,7},{6,4},{7,5},{8,10},{9,11},{10,... | collective-permute-start | bytes 331784 | tf_op jit(solution)/shard_map/ppermute | solution.py:34
  12.8 2.6 %collective-permute-start.2 = (bf16[64,864]{1,0:T(8,128)(2,1)S(1)}, bf16[64,864]{1,0:T(8,128)(2,1)S(1)}, u32[]{:S(2)}, u32[]{:S(2)}) collective-permute-start(bf16[64,864]{1,0:T(8,128)(2,1)S(1)} %maximum_select_fusion.refs_0_), channel_id=1, source_target_pairs={{0,4},{1,5},{2,6},{3,7},{4,0},{5,1},{6,2},{7,3},{8,12},{9,13},{10,... | collective-permute-start | bytes 331784 | tf_op jit(solution)/shard_map/ppermute | solution.py:34
  15.6 2.3 %collective-permute-done.1.refs_1_ = bf16[64,864]{1,0:T(8,128)(2,1)S(1)} collective-permute-done((bf16[64,864]{1,0:T(8,128)(2,1)S(1)}, bf16[64,864]{1,0:T(8,128)(2,1)S(1)}, u32[]{:S(2)}, u32[]{:S(2)}) %collective-permute-start.1) | collective-permute-done | bytes 110624 | tf_op jit(solution)/shard_map/ppermute | solution.py:34
  18.0 6.7 %collective-permute-done.2.refs_2_ = bf16[64,864]{1,0:T(8,128)(2,1)S(1)} collective-permute-done((bf16[64,864]{1,0:T(8,128)(2,1)S(1)}, bf16[64,864]{1,0:T(8,128)(2,1)S(1)}, u32[]{:S(2)}, u32[]{:S(2)}) %collective-permute-start.2) | collective-permute-done | bytes 110624 | tf_op jit(solution)/shard_map/ppermute | solution.py:34
  30.2 11.9 %shard_map.61 = (f32[128,256]{1,0:T(8,128)S(1)}, f32[864,256]{1,0:T(8,128)S(1)}, bf16[128,1024]{1,0:T(8,128)(2,1)S(1)}, bf16[128,1024]{1,0:T(8,128)(2,1)S(1)}, bf16[128,1024]{1,0:T(8,128)(2,1)S(1)}) custom-call(s32[1]{0:T(128)} %bitcast.1.core, bf16[288,768]{1,0:T(8,128)(2,1)S(1)} %shard_map.59.kernel, bf16[256,512]{1,0:T(8,128)(2,1)S(1)} %copy-done.7, ...), custom_call_target="tpu_custom_call" | custom-call | flops 5435817984 | bytes 7880708 | tf_op jit(solution)/shard_map/pallas_call | solution.py:396
  45.5 2.1 %shard_map.63 = (f32[128,256]{1,0:T(8,128)S(1)}, bf16[128,1024]{1,0:T(8,128)(2,1)S(1)}) custom-call(s32[1]{0:T(128)} %bitcast.1.core, bf16[288,768]{1,0:T(8,128)(2,1)S(1)} %shard_map.59.kernel, bf16[256,512]{1,0:T(8,128)(2,1)S(1)} %copy-done.8, bf16[160,1024]{1,0:T(8,128)(2,1)S(1)} %collective-permute-done.9.refs_0_, ...), custom_call_target="tpu_custom_call" | custom-call | flops 905969664 | bytes 2539524 | tf_op jit(solution)/shard_map/pallas_call | solution.py:396
  48.6 3.6 %collective-permute-start.22 = (f32[128,256]{1,0:T(8,128)S(1)}, f32[128,256]{1,0:T(8,128)S(1)}, u32[]{:S(2)}, u32[]{:S(2)}) collective-permute-start(f32[128,256]{1,0:T(8,128)S(1)} %get-tuple-element.46), channel_id=1, source_target_pairs={{0,6},{1,7},{2,4},{3,5},{4,2},{5,3},{6,0},{7,1},{8,14},{9,15},{10,... | collective-permute-start | bytes 393224 | tf_op jit(solution)/shard_map/ppermute | solution.py:34
  54.7 2.2 %collective-permute-done.22 = f32[128,256]{1,0:T(8,128)S(1)} collective-permute-done((f32[128,256]{1,0:T(8,128)S(1)}, f32[128,256]{1,0:T(8,128)S(1)}, u32[]{:S(2)}, u32[]{:S(2)}) %collective-permute-start.22) | collective-permute-done | bytes 131104 | tf_op jit(solution)/shard_map/ppermute | solution.py:34
  56.9 6.5 %collective-permute-done.21 = f32[128,256]{1,0:T(8,128)S(1)} collective-permute-done((f32[128,256]{1,0:T(8,128)S(1)}, f32[128,256]{1,0:T(8,128)S(1)}, u32[]{:S(2)}, u32[]{:S(2)}) %collective-permute-start.21) | collective-permute-done | bytes 131104 | tf_op jit(solution)/shard_map/ppermute | solution.py:34
  63.9 1.6 %shard_map.66.mine = f32[864,256]{1,0:T(8,128)S(1)} custom-call(bf16[256,2304]{1,0:T(8,128)(2,1)S(1)} %copy-done, bf16[128,1024]{1,0:T(8,128)(2,1)S(1)} %get-tuple-element.41.slopes, f32[864,256]{1,0:T(8,128)S(1)} %get-tuple-element.47.total_in, bf16[160,1024]{1,0:T(8,128)(2,1)S(1)} %collective-permute-done.9.refs_0_, ...), custom_call_target="tpu_custom_call", output_to_operand_aliasing={{}: (2, {})} | custom-call | flops 905969664 | bytes 4521984 | tf_op jit(solution)/shard_map/pallas_call | solution.py:396
  66.2 1.8 %shard_map.65 = f32[128,256]{1,0:T(8,128)S(1)} custom-call(s32[1]{0:T(128)} %bitcast.at, s32[1]{0:T(128)} %bitcast.1.core, bf16[128,1024]{1,0:T(8,128)(2,1)S(1)} %get-tuple-element.42.refs_0_, bf16[128,1024]{1,0:T(8,128)(2,1)S(1)} %collective-permute-done.13.refs_1_, bf16[128,1024]{1,0:T(8,128)(2,1)S(1)} %collective-permute-done.14.refs_2_, ...), custom_call_target="tpu_custom_call" | custom-call | flops 134217728 | bytes 2228232 | tf_op jit(solution)/shard_map/pallas_call | solution.py:396
  71.5 4.0 %shard_map.67.inverse = f32[256,256]{1,0:T(8,128)S(1)} custom-call(s32[1]{0:T(128)} %bitcast.1.core, f32[128,256]{1,0:T(8,128)S(1)} %add_add_fusion.mine, f32[128,256]{1,0:T(8,128)S(1)} %collective-permute-done.26.theirs), custom_call_target="tpu_custom_call" | custom-call | flops 3221225472 | bytes 524292 | tf_op jit(solution)/shard_map/pallas_call | solution.py:396
  76.2 2.5 %collective-permute-start.29 = (f32[32,256]{1,0:T(8,128)S(1)}, f32[32,256]{1,0:T(8,128)S(1)}, u32[]{:S(2)}, u32[]{:S(2)}) collective-permute-start(f32[32,256]{1,0:T(8,128)S(1)} %add_add_fusion.2), channel_id=1, source_target_pairs={{0,6},{1,7},{2,4},{3,5},{4,2},{5,3},{6,0},{7,1},{8,14},{9,15},{10,... | collective-permute-start | bytes 98312 | tf_op jit(solution)/shard_map/ppermute | solution.py:34
  78.8 1.9 %collective-permute-start.27 = (f32[32,256]{1,0:T(8,128)S(1)}, f32[32,256]{1,0:T(8,128)S(1)}, u32[]{:S(2)}, u32[]{:S(2)}) collective-permute-start(f32[32,256]{1,0:T(8,128)S(1)} %add_add_fusion.2), channel_id=1, source_target_pairs={{0,2},{1,3},{2,0},{3,1},{4,6},{5,7},{6,4},{7,5},{8,10},{9,11},{10,... | collective-permute-start | bytes 98312 | tf_op jit(solution)/shard_map/ppermute | solution.py:34
  80.7 2.1 %shard_map.64 = bf16[256,1024]{1,0:T(8,128)(2,1)} custom-call(s32[1]{0:T(128)} %bitcast.at, s32[1]{0:T(128)} %bitcast.1.core, bf16[128,1024]{1,0:T(8,128)(2,1)S(1)} %get-tuple-element.42.refs_0_, bf16[128,1024]{1,0:T(8,128)(2,1)S(1)} %collective-permute-done.13.refs_1_, bf16[128,1024]{1,0:T(8,128)(2,1)S(1)} %collective-permute-done.14.refs_2_, ...), custom_call_target="tpu_custom_call" | custom-call | bytes 2621448 | tf_op jit(solution)/shard_map/pallas_call | solution.py:396
  86.5 1.6 %collective-permute-start.33 = (f32[32,256]{1,0:T(8,128)S(1)}, f32[32,256]{1,0:T(8,128)S(1)}, u32[]{:S(2)}, u32[]{:S(2)}) collective-permute-start(f32[32,256]{1,0:T(8,128)S(1)} %add_add_fusion.1), channel_id=1, source_target_pairs={{0,24},{1,25},{2,26},{3,27},{4,28},{5,29},{6,30},{7,31},{8,16},{9,... | collective-permute-start | bytes 98312 | tf_op jit(solution)/shard_map/ppermute | solution.py:34
  88.2 1.9 %collective-permute-start.37 = (bf16[2,32,864]{2,1,0:T(8,128)(2,1)S(1)}, bf16[2,32,864]{2,1,0:T(8,128)(2,1)S(1)}, u32[]{:S(2)}, u32[]{:S(2)}) collective-permute-start(bf16[2,32,864]{2,1,0:T(8,128)(2,1)S(1)} %get-tuple-element.55), channel_id=1, source_target_pairs={{0,6},{1,7},{2,4},{3,5},{4,2},{5,3},{6,0},{7,1},{8,14},{9,15},{10,... | collective-permute-start | bytes 331784 | tf_op jit(solution)/shard_map/ppermute | solution.py:34
  90.7 1.9 %collective-permute-start.35 = (bf16[2,32,864]{2,1,0:T(8,128)(2,1)S(1)}, bf16[2,32,864]{2,1,0:T(8,128)(2,1)S(1)}, u32[]{:S(2)}, u32[]{:S(2)}) collective-permute-start(bf16[2,32,864]{2,1,0:T(8,128)(2,1)S(1)} %get-tuple-element.54), channel_id=1, source_target_pairs={{0,2},{1,3},{2,0},{3,1},{4,6},{5,7},{6,4},{7,5},{8,10},{9,11},{10,... | collective-permute-start | bytes 331784 | tf_op jit(solution)/shard_map/ppermute | solution.py:34
  92.8 2.3 %collective-permute-done.37 = bf16[2,32,864]{2,1,0:T(8,128)(2,1)S(1)} collective-permute-done((bf16[2,32,864]{2,1,0:T(8,128)(2,1)S(1)}, bf16[2,32,864]{2,1,0:T(8,128)(2,1)S(1)}, u32[]{:S(2)}, u32[]{:S(2)}) %collective-permute-start.37) | collective-permute-done | bytes 110624 | tf_op jit(solution)/shard_map/ppermute | solution.py:34
  95.0 3.5 %collective-permute-done.36 = bf16[2,32,864]{2,1,0:T(8,128)(2,1)S(1)} collective-permute-done((bf16[2,32,864]{2,1,0:T(8,128)(2,1)S(1)}, bf16[2,32,864]{2,1,0:T(8,128)(2,1)S(1)}, u32[]{:S(2)}, u32[]{:S(2)}) %collective-permute-start.36) | collective-permute-done | bytes 110624 | tf_op jit(solution)/shard_map/ppermute | solution.py:34
  102.1 4.0 %shard_map.69.inverse = f32[256,256]{1,0:T(8,128)S(1)} custom-call(s32[1]{0:T(128)} %bitcast.1.core, f32[128,256]{1,0:T(8,128)S(1)} %constant_dynamic-update-slice_fusion.mine, f32[128,256]{1,0:T(8,128)S(1)} %collective-permute-done.34.theirs), custom_call_target="tpu_custom_call" | custom-call | flops 3221225472 | bytes 524292 | tf_op jit(solution)/shard_map/pallas_call | solution.py:396
  107.1 2.7 %collective-permute-done.39.refs_2_ = f32[2,32,864]{2,1,0:T(8,128)S(1)} collective-permute-done((f32[2,32,864]{2,1,0:T(8,128)S(1)}, f32[2,32,864]{2,1,0:T(8,128)S(1)}, u32[]{:S(2)}, u32[]{:S(2)}) %collective-permute-start.39) | collective-permute-done | bytes 221216 | tf_op jit(solution)/shard_map/ppermute | solution.py:34
  109.8 2.0 %shard_map.70 = f32[864,256]{1,0:T(8,128)} custom-call(s32[1]{0:T(128)} %bitcast.at, f32[256,256]{1,0:T(8,128)S(1)} %shard_map.69.inverse, f32[2,32,864]{2,1,0:T(8,128)S(1)} %convert_add_fusion.refs_0_, f32[2,32,864]{2,1,0:T(8,128)S(1)} %collective-permute-done.38.refs_1_, f32[2,32,864]{2,1,0:T(8,128)S(1)} %collective-permute-done.39.refs_2_, ...), custom_call_target="tpu_custom_call" | custom-call | flops 679477248 | bytes 2031620 | tf_op jit(solution)/shard_map/pallas_call | solution.py:396
  (105 shorter events, 34.6 us)
Async XLA Ops:
  3.7 20.9 %collective-permute-start.4 = (bf16[384,1024]{1,0:T(8,128)(2,1)S(1)}, bf16[384,1024]{1,0:T(8,128)(2,1)S(1)}, u32[]{:S(2)}, u32[]{:S(2)}) collective-permute-start(bf16[384,1024]{1,0:T(8,128)(2,1)S(1)} %get-tuple-element.29), channel_id=1, source_target_pairs={{0,8},{1,9},{2,10},{3,11},{4,12},{5,13},{6,14},{7,15},{8,0},{9,1},... | collective-permute-start | bytes 2359304 | tf_op jit(solution)/shard_map/ppermute | solution.py:34
  6.8 17.9 %collective-permute-start.5 = (bf16[320,1024]{1,0:T(8,128)(2,1)S(1)}, bf16[320,1024]{1,0:T(8,128)(2,1)S(1)}, u32[]{:S(2)}, u32[]{:S(2)}) collective-permute-start(bf16[320,1024]{1,0:T(8,128)(2,1)S(1)} %get-tuple-element.30), channel_id=1, source_target_pairs={{0,16},{1,17},{2,18},{3,19},{4,20},{5,21},{6,22},{7,23},{8,24},{9,... | collective-permute-start | bytes 1966088 | tf_op jit(solution)/shard_map/ppermute | solution.py:34
  12.8 11.8 %collective-permute-start.2 = (bf16[64,864]{1,0:T(8,128)(2,1)S(1)}, bf16[64,864]{1,0:T(8,128)(2,1)S(1)}, u32[]{:S(2)}, u32[]{:S(2)}) collective-permute-start(bf16[64,864]{1,0:T(8,128)(2,1)S(1)} %maximum_select_fusion.refs_0_), channel_id=1, source_target_pairs={{0,4},{1,5},{2,6},{3,7},{4,0},{5,1},{6,2},{7,3},{8,12},{9,13},{10,... | collective-permute-start | bytes 331784 | tf_op jit(solution)/shard_map/ppermute | solution.py:34
  15.4 9.3 %collective-permute-start.3 = (bf16[64,864]{1,0:T(8,128)(2,1)S(1)}, bf16[64,864]{1,0:T(8,128)(2,1)S(1)}, u32[]{:S(2)}, u32[]{:S(2)}) collective-permute-start(bf16[64,864]{1,0:T(8,128)(2,1)S(1)} %maximum_select_fusion.refs_0_), channel_id=1, source_target_pairs={{0,6},{1,7},{2,4},{3,5},{4,2},{5,3},{6,0},{7,1},{8,14},{9,15},{10,... | collective-permute-start | bytes 331784 | tf_op jit(solution)/shard_map/ppermute | solution.py:34
  25.7 16.4 %collective-permute-start.9 = (bf16[160,1024]{1,0:T(8,128)(2,1)S(1)}, bf16[160,1024]{1,0:T(8,128)(2,1)S(1)}, u32[]{:S(2)}, u32[]{:S(2)}) collective-permute-start(bf16[160,1024]{1,0:T(8,128)(2,1)S(1)} %get-tuple-element.35), channel_id=1, source_target_pairs={{0,16},{1,17},{2,18},{3,19},{4,20},{5,21},{6,22},{7,23},{8,24},{9,... | collective-permute-start | bytes 983048 | tf_op jit(solution)/shard_map/ppermute | solution.py:34
  27.0 15.1 %collective-permute-start.10 = (bf16[160,1024]{1,0:T(8,128)(2,1)S(1)}, bf16[160,1024]{1,0:T(8,128)(2,1)S(1)}, u32[]{:S(2)}, u32[]{:S(2)}) collective-permute-start(bf16[160,1024]{1,0:T(8,128)(2,1)S(1)} %get-tuple-element.38), channel_id=1, source_target_pairs={{0,8},{1,9},{2,10},{3,11},{4,12},{5,13},{6,14},{7,15},{8,0},{9,1},... | collective-permute-start | bytes 983048 | tf_op jit(solution)/shard_map/ppermute | solution.py:34
  42.7 12.1 %collective-permute-start.14 = (bf16[128,1024]{1,0:T(8,128)(2,1)S(1)}, bf16[128,1024]{1,0:T(8,128)(2,1)S(1)}, u32[]{:S(2)}, u32[]{:S(2)}) collective-permute-start(bf16[128,1024]{1,0:T(8,128)(2,1)S(1)} %get-tuple-element.36), channel_id=1, source_target_pairs={{0,16},{1,17},{2,18},{3,19},{4,20},{5,21},{6,22},{7,23},{8,24},{9,... | collective-permute-start | bytes 786440 | tf_op jit(solution)/shard_map/ppermute | solution.py:34
  44.0 9.2 %collective-permute-start.13 = (bf16[128,1024]{1,0:T(8,128)(2,1)S(1)}, bf16[128,1024]{1,0:T(8,128)(2,1)S(1)}, u32[]{:S(2)}, u32[]{:S(2)}) collective-permute-start(bf16[128,1024]{1,0:T(8,128)(2,1)S(1)} %get-tuple-element.43), channel_id=1, source_target_pairs={{0,8},{1,9},{2,10},{3,11},{4,12},{5,13},{6,14},{7,15},{8,0},{9,1},... | collective-permute-start | bytes 786440 | tf_op jit(solution)/shard_map/ppermute | solution.py:34
  47.6 15.8 %collective-permute-start.15 = (bf16[128,1024]{1,0:T(8,128)(2,1)S(1)}, bf16[128,1024]{1,0:T(8,128)(2,1)S(1)}, u32[]{:S(2)}, u32[]{:S(2)}) collective-permute-start(bf16[128,1024]{1,0:T(8,128)(2,1)S(1)} %get-tuple-element.41.slopes), channel_id=1, source_target_pairs={{0,24},{1,25},{2,26},{3,27},{4,28},{5,29},{6,30},{7,31},{8,16},{9,... | collective-permute-start | bytes 786440 | tf_op jit(solution)/shard_map/ppermute | solution.py:34
  48.6 8.2 %collective-permute-start.22 = (f32[128,256]{1,0:T(8,128)S(1)}, f32[128,256]{1,0:T(8,128)S(1)}, u32[]{:S(2)}, u32[]{:S(2)}) collective-permute-start(f32[128,256]{1,0:T(8,128)S(1)} %get-tuple-element.46), channel_id=1, source_target_pairs={{0,6},{1,7},{2,4},{3,5},{4,2},{5,3},{6,0},{7,1},{8,14},{9,15},{10,... | collective-permute-start | bytes 393224 | tf_op jit(solution)/shard_map/ppermute | solution.py:34
  52.2 11.2 %collective-permute-start.21 = (f32[128,256]{1,0:T(8,128)S(1)}, f32[128,256]{1,0:T(8,128)S(1)}, u32[]{:S(2)}, u32[]{:S(2)}) collective-permute-start(f32[128,256]{1,0:T(8,128)S(1)} %get-tuple-element.46), channel_id=1, source_target_pairs={{0,4},{1,5},{2,6},{3,7},{4,0},{5,1},{6,2},{7,3},{8,12},{9,13},{10,... | collective-permute-start | bytes 393224 | tf_op jit(solution)/shard_map/ppermute | solution.py:34
  53.1 12.4 %collective-permute-start.20 = (f32[128,256]{1,0:T(8,128)S(1)}, f32[128,256]{1,0:T(8,128)S(1)}, u32[]{:S(2)}, u32[]{:S(2)}) collective-permute-start(f32[128,256]{1,0:T(8,128)S(1)} %get-tuple-element.46), channel_id=1, source_target_pairs={{0,2},{1,3},{2,0},{3,1},{4,6},{5,7},{6,4},{7,5},{8,10},{9,11},{10,... | collective-permute-start | bytes 393224 | tf_op jit(solution)/shard_map/ppermute | solution.py:34
  54.7 11.0 %collective-permute-start.16 = (bf16[128,1024]{1,0:T(8,128)(2,1)S(1)}, bf16[128,1024]{1,0:T(8,128)(2,1)S(1)}, u32[]{:S(2)}, u32[]{:S(2)}) collective-permute-start(bf16[128,1024]{1,0:T(8,128)(2,1)S(1)} %get-tuple-element.42.refs_0_), channel_id=1, source_target_pairs={{0,1},{1,0},{2,3},{3,2},{4,5},{5,4},{6,7},{7,6},{8,9},{9,8},{10,11... | collective-permute-start | bytes 786440 | tf_op jit(solution)/shard_map/ppermute | solution.py:34
  56.9 9.3 %collective-permute-start.17 = (bf16[128,1024]{1,0:T(8,128)(2,1)S(1)}, bf16[128,1024]{1,0:T(8,128)(2,1)}, u32[]{:S(2)}, u32[]{:S(2)}) collective-permute-start(bf16[128,1024]{1,0:T(8,128)(2,1)S(1)} %collective-permute-done.13.refs_1_), channel_id=1, source_target_pairs={{0,1},{1,0},{2,3},{3,2},{4,5},{5,4},{6,7},{7,6},{8,9},{9,8},{10,11... | collective-permute-start | bytes 786440 | tf_op jit(solution)/shard_map/ppermute | solution.py:34
  65.7 17.9 %collective-permute-start.30 = (f32[864,256]{1,0:T(8,128)S(1)}, f32[864,256]{1,0:T(8,128)S(1)}, u32[]{:S(2)}, u32[]{:S(2)}) collective-permute-start(f32[864,256]{1,0:T(8,128)S(1)} %shard_map.66.mine), channel_id=1, source_target_pairs={{0,1},{1,0},{2,3},{3,2},{4,5},{5,4},{6,7},{7,6},{8,9},{9,8},{10,11... | collective-permute-start | bytes 2654216 | tf_op jit(solution)/shard_map/ppermute | solution.py:34
  68.0 8.2 %collective-permute-start.25 = (f32[32,256]{1,0:T(8,128)S(1)}, f32[32,256]{1,0:T(8,128)S(1)}, u32[]{:S(2)}, u32[]{:S(2)}) collective-permute-start(f32[32,256]{1,0:T(8,128)S(1)} %get-tuple-element.60), channel_id=1, source_target_pairs={{0,24},{1,25},{2,26},{3,27},{4,28},{5,29},{6,30},{7,31},{8,16},{9,... | collective-permute-start | bytes 98312 | tf_op jit(solution)/shard_map/ppermute | solution.py:34
  85.2 7.5 %collective-permute-start.32 = (f32[32,256]{1,0:T(8,128)S(1)}, f32[32,256]{1,0:T(8,128)S(1)}, u32[]{:S(2)}, u32[]{:S(2)}) collective-permute-start(f32[32,256]{1,0:T(8,128)S(1)} %add_add_fusion.1), channel_id=1, source_target_pairs={{0,16},{1,17},{2,18},{3,19},{4,20},{5,21},{6,22},{7,23},{8,24},{9,... | collective-permute-start | bytes 98312 | tf_op jit(solution)/shard_map/ppermute | solution.py:34
  88.2 6.8 %collective-permute-start.37 = (bf16[2,32,864]{2,1,0:T(8,128)(2,1)S(1)}, bf16[2,32,864]{2,1,0:T(8,128)(2,1)S(1)}, u32[]{:S(2)}, u32[]{:S(2)}) collective-permute-start(bf16[2,32,864]{2,1,0:T(8,128)(2,1)S(1)} %get-tuple-element.55), channel_id=1, source_target_pairs={{0,6},{1,7},{2,4},{3,5},{4,2},{5,3},{6,0},{7,1},{8,14},{9,15},{10,... | collective-permute-start | bytes 331784 | tf_op jit(solution)/shard_map/ppermute | solution.py:34
  90.0 8.5 %collective-permute-start.36 = (bf16[2,32,864]{2,1,0:T(8,128)(2,1)S(1)}, bf16[2,32,864]{2,1,0:T(8,128)(2,1)S(1)}, u32[]{:S(2)}, u32[]{:S(2)}) collective-permute-start(bf16[2,32,864]{2,1,0:T(8,128)(2,1)S(1)} %get-tuple-element.56), channel_id=1, source_target_pairs={{0,4},{1,5},{2,6},{3,7},{4,0},{5,1},{6,2},{7,3},{8,12},{9,13},{10,... | collective-permute-start | bytes 331784 | tf_op jit(solution)/shard_map/ppermute | solution.py:34
  90.7 7.8 %collective-permute-start.35 = (bf16[2,32,864]{2,1,0:T(8,128)(2,1)S(1)}, bf16[2,32,864]{2,1,0:T(8,128)(2,1)S(1)}, u32[]{:S(2)}, u32[]{:S(2)}) collective-permute-start(bf16[2,32,864]{2,1,0:T(8,128)(2,1)S(1)} %get-tuple-element.54), channel_id=1, source_target_pairs={{0,2},{1,3},{2,0},{3,1},{4,6},{5,7},{6,4},{7,5},{8,10},{9,11},{10,... | collective-permute-start | bytes 331784 | tf_op jit(solution)/shard_map/ppermute | solution.py:34
  92.7 9.5 %collective-permute-start.34 = (f32[128,256]{1,0:T(8,128)S(1)}, f32[128,256]{1,0:T(8,128)S(1)}, u32[]{:S(2)}, u32[]{:S(2)}) collective-permute-start(f32[128,256]{1,0:T(8,128)S(1)} %constant_dynamic-update-slice_fusion.mine), channel_id=1, source_target_pairs={{0,1},{1,0},{2,3},{3,2},{4,5},{5,4},{6,7},{7,6},{8,9},{9,8},{10,11... | collective-permute-start | bytes 393224 | tf_op jit(solution)/shard_map/ppermute | solution.py:34
  98.6 8.5 %collective-permute-start.38 = (f32[2,32,864]{2,1,0:T(8,128)S(1)}, f32[2,32,864]{2,1,0:T(8,128)S(1)}, u32[]{:S(2)}, u32[]{:S(2)}) collective-permute-start(f32[2,32,864]{2,1,0:T(8,128)S(1)} %convert_add_fusion.refs_0_), channel_id=1, source_target_pairs={{0,8},{1,9},{2,10},{3,11},{4,12},{5,13},{6,14},{7,15},{8,0},{9,1},... | collective-permute-start | bytes 663560 | tf_op jit(solution)/shard_map/ppermute | solution.py:34
  99.2 10.6 %collective-permute-start.39 = (f32[2,32,864]{2,1,0:T(8,128)S(1)}, f32[2,32,864]{2,1,0:T(8,128)S(1)}, u32[]{:S(2)}, u32[]{:S(2)}) collective-permute-start(f32[2,32,864]{2,1,0:T(8,128)S(1)} %convert_add_fusion.refs_0_), channel_id=1, source_target_pairs={{0,16},{1,17},{2,18},{3,19},{4,20},{5,21},{6,22},{7,23},{8,24},{9,... | collective-permute-start | bytes 663560 | tf_op jit(solution)/shard_map/ppermute | solution.py:34
  100.6 9.3 %collective-permute-start.40 = (f32[2,32,864]{2,1,0:T(8,128)S(1)}, f32[2,32,864]{2,1,0:T(8,128)S(1)}, u32[]{:S(2)}, u32[]{:S(2)}) collective-permute-start(f32[2,32,864]{2,1,0:T(8,128)S(1)} %convert_add_fusion.refs_0_), channel_id=1, source_target_pairs={{0,24},{1,25},{2,26},{3,27},{4,28},{5,29},{6,30},{7,31},{8,16},{9,... | collective-permute-start | bytes 663560 | tf_op jit(solution)/shard_map/ppermute | solution.py:34
  (26 other events, 110.4 us)

commit v2 on v1

--- a/solution.py
+++ b/solution.py
@@ -58,10 +58,13 @@
     right_high = right.astype(jnp.bfloat16)
     right_low = (right - right_high.astype(jnp.float32)).astype(jnp.bfloat16)
 
-    def dot(a, b):
-        return lax.dot_general(a, b, dims, preferred_element_type=jnp.float32)
-
-    return dot(left_high, right_high) + (dot(left_high, right_low) + dot(left_low, right_high))
+    (left_dim,), (right_dim,) = dims[0]
+    return lax.dot_general(
+        jnp.concatenate([left_high, left_low, left_high], axis=left_dim),
+        jnp.concatenate([right_high, right_high, right_low], axis=right_dim),
+        dims,
+        preferred_element_type=jnp.float32,
+    )
 
 
 def shift_matrices():
@@ -384,7 +387,7 @@
             for tap in range(taps):
                 rows[tap * own_rows : (tap + 1) * own_rows, block : block + out] = pieces[step][
                     core, :, tap * out : (tap + 1) * out
-                ]
+                ].astype(jnp.float32)
     result[...] = dot3(rows[...], factor[...]) * scale
 
 
@@ -520,7 +523,7 @@
         swap(part, dp=step) for step, part in enumerate(results) if step > 0
     ]
     back = [after(part, result) for part in back] + [swap(result, dp=planes - 1)]
-    theirs = [swap(result, core=1) for result in back]
+    theirs = [swap(after(part, total), core=1) for part in back]
 
     part = a_half
     for step in range(1, pairs):
@@ -581,6 +584,7 @@
 
     inv_g = inverse_of(g_half)
 
+    block = block.astype(bf16)
     pieces = [block] + [swap(block, dp=step) for step in range(1, planes)]
     (update,) = call(
         functools.partial(update_kernel, planes, taps, out, 1.0 / math.sqrt(count)),

time: 112 us -> 107 us (0.955)
  waiting for transfers between devices: 30.4 us -> 26 us
    ppermute x41, waiting for transfers between devices: 30.4 us -> 26 us  [exchange(): return lax.ppermute(x, AXES, perm)]
    unnamed x18 -> x12, local copies, waits for them, and re-layouts: 3.87 us -> 3.17 us
  transfers between devices with their start and end apart: 41 -> 41, of which waited for: 13 -> 12; matrix products, arithmetic and copies ran while one was open for 2% -> 2% of each run, Pallas kernels for 25% -> 25%
where the time goes in v2:
time: 107 us; the launch traced here: 106 us
  starting transfers between devices  43 us (40%)
  Pallas kernels  31.1 us (29%)
  waiting for transfers between devices  26 us (24%)
  local copies, waits for them, and re-layouts  5.15 us (5%)
    ppermute x41, starting transfers between devices, exchange(): return lax.ppermute(x, AXES, perm)  43 us
    pallas_call x12, Pallas kernels, call(): pl.pallas_call(kernel, out_shape=tuple(shapes), in_specs=in_specs, out_sp...  31.1 us
    ppermute x41, waiting for transfers between devices, exchange(): return lax.ppermute(x, AXES, perm)  26 us
    unnamed x12, local copies, waits for them, and re-layouts  3.17 us
  transfers between devices with their start and end apart: 41, of which 12 were waited for; matrix products, arithmetic and copies ran while one was open for 2% of the time, Pallas kernels for 25%

profile of v2, /device:TPU:0, one launch (start us, length us, event | category | flops | bytes accessed | tf_op | source)
XLA Modules:
  0.0 106.4 jit_solution(12445417640176075008)
XLA Ops:
  3.7 3.0 %collective-permute-start.4 = (bf16[384,1024]{1,0:T(8,128)(2,1)S(1)}, bf16[384,1024]{1,0:T(8,128)(2,1)S(1)}, u32[]{:S(2)}, u32[]{:S(2)}) collective-permute-start(bf16[384,1024]{1,0:T(8,128)(2,1)S(1)} %get-tuple-element.33), channel_id=1, source_target_pairs={{0,8},{1,9},{2,10},{3,11},{4,12},{5,13},{6,14},{7,15},{8,0},{9,1},... | collective-permute-start | bytes 2359304 | tf_op jit(solution)/shard_map/ppermute | solution.py:34
  11.2 1.6 %collective-permute-start.1 = (bf16[64,864]{1,0:T(8,128)(2,1)S(1)}, bf16[64,864]{1,0:T(8,128)(2,1)S(1)}, u32[]{:S(2)}, u32[]{:S(2)}) collective-permute-start(bf16[64,864]{1,0:T(8,128)(2,1)S(1)} %maximum_select_fusion.refs_0_), channel_id=1, source_target_pairs={{0,2},{1,3},{2,0},{3,1},{4,6},{5,7},{6,4},{7,5},{8,10},{9,11},{10,... | collective-permute-start | bytes 331784 | tf_op jit(solution)/shard_map/ppermute | solution.py:34
  12.8 2.6 %collective-permute-start.2 = (bf16[64,864]{1,0:T(8,128)(2,1)S(1)}, bf16[64,864]{1,0:T(8,128)(2,1)S(1)}, u32[]{:S(2)}, u32[]{:S(2)}) collective-permute-start(bf16[64,864]{1,0:T(8,128)(2,1)S(1)} %maximum_select_fusion.refs_0_), channel_id=1, source_target_pairs={{0,4},{1,5},{2,6},{3,7},{4,0},{5,1},{6,2},{7,3},{8,12},{9,13},{10,... | collective-permute-start | bytes 331784 | tf_op jit(solution)/shard_map/ppermute | solution.py:34
  15.6 2.3 %collective-permute-done.1.refs_1_ = bf16[64,864]{1,0:T(8,128)(2,1)S(1)} collective-permute-done((bf16[64,864]{1,0:T(8,128)(2,1)S(1)}, bf16[64,864]{1,0:T(8,128)(2,1)S(1)}, u32[]{:S(2)}, u32[]{:S(2)}) %collective-permute-start.1) | collective-permute-done | bytes 110624 | tf_op jit(solution)/shard_map/ppermute | solution.py:34
  18.0 6.7 %collective-permute-done.2.refs_2_ = bf16[64,864]{1,0:T(8,128)(2,1)S(1)} collective-permute-done((bf16[64,864]{1,0:T(8,128)(2,1)S(1)}, bf16[64,864]{1,0:T(8,128)(2,1)S(1)}, u32[]{:S(2)}, u32[]{:S(2)}) %collective-permute-start.2) | collective-permute-done | bytes 110624 | tf_op jit(solution)/shard_map/ppermute | solution.py:34
  30.2 11.9 %shard_map.61 = (f32[128,256]{1,0:T(8,128)S(1)}, f32[864,256]{1,0:T(8,128)S(1)}, bf16[128,1024]{1,0:T(8,128)(2,1)S(1)}, bf16[128,1024]{1,0:T(8,128)(2,1)S(1)}, bf16[128,1024]{1,0:T(8,128)(2,1)S(1)}) custom-call(s32[1]{0:T(128)} %bitcast.1.core, bf16[288,768]{1,0:T(8,128)(2,1)S(1)} %shard_map.59.kernel, bf16[256,512]{1,0:T(8,128)(2,1)S(1)} %copy-done.5, ...), custom_call_target="tpu_custom_call" | custom-call | flops 5435817984 | bytes 7880708 | tf_op jit(solution)/shard_map/pallas_call | solution.py:399
  45.4 2.0 %shard_map.63 = (f32[128,256]{1,0:T(8,128)S(1)}, bf16[128,1024]{1,0:T(8,128)(2,1)S(1)}) custom-call(s32[1]{0:T(128)} %bitcast.1.core, bf16[288,768]{1,0:T(8,128)(2,1)S(1)} %shard_map.59.kernel, bf16[256,512]{1,0:T(8,128)(2,1)S(1)} %copy-done.5, bf16[160,1024]{1,0:T(8,128)(2,1)S(1)} %collective-permute-done.9.refs_0_, ...), custom_call_target="tpu_custom_call" | custom-call | flops 905969664 | bytes 2539524 | tf_op jit(solution)/shard_map/pallas_call | solution.py:399
  48.5 3.6 %collective-permute-start.22 = (f32[128,256]{1,0:T(8,128)S(1)}, f32[128,256]{1,0:T(8,128)S(1)}, u32[]{:S(2)}, u32[]{:S(2)}) collective-permute-start(f32[128,256]{1,0:T(8,128)S(1)} %get-tuple-element.55), channel_id=1, source_target_pairs={{0,6},{1,7},{2,4},{3,5},{4,2},{5,3},{6,0},{7,1},{8,14},{9,15},{10,... | collective-permute-start | bytes 393224 | tf_op jit(solution)/shard_map/ppermute | solution.py:34
  52.1 1.6 %collective-permute-start.20 = (f32[128,256]{1,0:T(8,128)S(1)}, f32[128,256]{1,0:T(8,128)S(1)}, u32[]{:S(2)}, u32[]{:S(2)}) collective-permute-start(f32[128,256]{1,0:T(8,128)S(1)} %get-tuple-element.55), channel_id=1, source_target_pairs={{0,2},{1,3},{2,0},{3,1},{4,6},{5,7},{6,4},{7,5},{8,10},{9,11},{10,... | collective-permute-start | bytes 393224 | tf_op jit(solution)/shard_map/ppermute | solution.py:34
  53.7 3.9 %collective-permute-done.14.refs_2_ = bf16[128,1024]{1,0:T(8,128)(2,1)S(1)} collective-permute-done((bf16[128,1024]{1,0:T(8,128)(2,1)S(1)}, bf16[128,1024]{1,0:T(8,128)(2,1)S(1)}, u32[]{:S(2)}, u32[]{:S(2)}) %collective-permute-start.14) | collective-permute-done | bytes 262176 | tf_op jit(solution)/shard_map/ppermute | solution.py:34
  57.7 1.6 %shard_map.64.mine = f32[864,256]{1,0:T(8,128)S(1)} custom-call(bf16[256,2304]{1,0:T(8,128)(2,1)S(1)} %copy-done, bf16[128,1024]{1,0:T(8,128)(2,1)S(1)} %get-tuple-element.45.slopes, f32[864,256]{1,0:T(8,128)S(1)} %get-tuple-element.50.total_in, bf16[160,1024]{1,0:T(8,128)(2,1)S(1)} %collective-permute-done.9.refs_0_, ...), custom_call_target="tpu_custom_call", output_to_operand_aliasing={{}: (2, {})} | custom-call | flops 905969664 | bytes 4521984 | tf_op jit(solution)/shard_map/pallas_call | solution.py:399
  59.9 3.4 %collective-permute-done.21 = f32[128,256]{1,0:T(8,128)S(1)} collective-permute-done((f32[128,256]{1,0:T(8,128)S(1)}, f32[128,256]{1,0:T(8,128)S(1)}, u32[]{:S(2)}, u32[]{:S(2)}) %collective-permute-start.21) | collective-permute-done | bytes 131104 | tf_op jit(solution)/shard_map/ppermute | solution.py:34
  69.4 4.0 %shard_map.67.inverse = f32[256,256]{1,0:T(8,128)S(1)} custom-call(s32[1]{0:T(128)} %bitcast.1.core, f32[128,256]{1,0:T(8,128)S(1)} %add_add_fusion.mine, f32[128,256]{1,0:T(8,128)S(1)} %collective-permute-done.26.theirs), custom_call_target="tpu_custom_call" | custom-call | flops 3221225472 | bytes 524292 | tf_op jit(solution)/shard_map/pallas_call | solution.py:399
  73.5 2.6 %collective-permute-start.29 = (f32[32,256]{1,0:T(8,128)S(1)}, f32[32,256]{1,0:T(8,128)S(1)}, u32[]{:S(2)}, u32[]{:S(2)}) collective-permute-start(f32[32,256]{1,0:T(8,128)S(1)} %add_add_fusion.2), channel_id=1, source_target_pairs={{0,6},{1,7},{2,4},{3,5},{4,2},{5,3},{6,0},{7,1},{8,14},{9,15},{10,... | collective-permute-start | bytes 98312 | tf_op jit(solution)/shard_map/ppermute | solution.py:34
  76.0 1.9 %collective-permute-start.27 = (f32[32,256]{1,0:T(8,128)S(1)}, f32[32,256]{1,0:T(8,128)S(1)}, u32[]{:S(2)}, u32[]{:S(2)}) collective-permute-start(f32[32,256]{1,0:T(8,128)S(1)} %add_add_fusion.2), channel_id=1, source_target_pairs={{0,2},{1,3},{2,0},{3,1},{4,6},{5,7},{6,4},{7,5},{8,10},{9,11},{10,... | collective-permute-start | bytes 98312 | tf_op jit(solution)/shard_map/ppermute | solution.py:34
  80.9 2.1 %shard_map.68 = (f32[2,128,864]{2,1,0:T(8,128)S(1)}, bf16[2,128,864]{2,1,0:T(8,128)(2,1)S(1)}) custom-call(s32[1]{0:T(128)} %bitcast.1.core, f32[256,256]{1,0:T(8,128)S(1)} %shard_map.67.inverse, f32[864,256]{1,0:T(8,128)S(1)} %shard_map.64.mine, f32[864,256]{1,0:T(8,128)} %collective-permute-done.30.theirs), custom_call_target="tpu_custom_call" | custom-call | flops 339738624 | bytes 3358724 | tf_op jit(solution)/shard_map/pallas_call | solution.py:399
  84.9 1.6 %collective-permute-start.33 = (f32[32,256]{1,0:T(8,128)S(1)}, f32[32,256]{1,0:T(8,128)S(1)}, u32[]{:S(2)}, u32[]{:S(2)}) collective-permute-start(f32[32,256]{1,0:T(8,128)S(1)} %add_add_fusion.1), channel_id=1, source_target_pairs={{0,24},{1,25},{2,26},{3,27},{4,28},{5,29},{6,30},{7,31},{8,16},{9,... | collective-permute-start | bytes 98312 | tf_op jit(solution)/shard_map/ppermute | solution.py:34
  86.6 1.9 %collective-permute-start.37 = (bf16[2,32,864]{2,1,0:T(8,128)(2,1)S(1)}, bf16[2,32,864]{2,1,0:T(8,128)(2,1)S(1)}, u32[]{:S(2)}, u32[]{:S(2)}) collective-permute-start(bf16[2,32,864]{2,1,0:T(8,128)(2,1)S(1)} %get-tuple-element.63), channel_id=1, source_target_pairs={{0,6},{1,7},{2,4},{3,5},{4,2},{5,3},{6,0},{7,1},{8,14},{9,15},{10,... | collective-permute-start | bytes 331784 | tf_op jit(solution)/shard_map/ppermute | solution.py:34
  89.1 1.9 %collective-permute-start.35 = (bf16[2,32,864]{2,1,0:T(8,128)(2,1)S(1)}, bf16[2,32,864]{2,1,0:T(8,128)(2,1)S(1)}, u32[]{:S(2)}, u32[]{:S(2)}) collective-permute-start(bf16[2,32,864]{2,1,0:T(8,128)(2,1)S(1)} %get-tuple-element.62), channel_id=1, source_target_pairs={{0,2},{1,3},{2,0},{3,1},{4,6},{5,7},{6,4},{7,5},{8,10},{9,11},{10,... | collective-permute-start | bytes 331784 | tf_op jit(solution)/shard_map/ppermute | solution.py:34
  91.2 2.3 %collective-permute-done.37 = bf16[2,32,864]{2,1,0:T(8,128)(2,1)S(1)} collective-permute-done((bf16[2,32,864]{2,1,0:T(8,128)(2,1)S(1)}, bf16[2,32,864]{2,1,0:T(8,128)(2,1)S(1)}, u32[]{:S(2)}, u32[]{:S(2)}) %collective-permute-start.37) | collective-permute-done | bytes 110624 | tf_op jit(solution)/shard_map/ppermute | solution.py:34
  93.5 3.5 %collective-permute-done.36 = bf16[2,32,864]{2,1,0:T(8,128)(2,1)S(1)} collective-permute-done((bf16[2,32,864]{2,1,0:T(8,128)(2,1)S(1)}, bf16[2,32,864]{2,1,0:T(8,128)(2,1)S(1)}, u32[]{:S(2)}, u32[]{:S(2)}) %collective-permute-start.36) | collective-permute-done | bytes 110624 | tf_op jit(solution)/shard_map/ppermute | solution.py:34
  99.0 1.6 %collective-permute-start.40 = (bf16[2,32,864]{2,1,0:T(8,128)(2,1)S(1)}, bf16[2,32,864]{2,1,0:T(8,128)(2,1)S(1)}, u32[]{:S(2)}, u32[]{:S(2)}) collective-permute-start(bf16[2,32,864]{2,1,0:T(8,128)(2,1)S(1)} %add_convert_fusion.refs_0_), channel_id=1, source_target_pairs={{0,24},{1,25},{2,26},{3,27},{4,28},{5,29},{6,30},{7,31},{8,16},{9,... | collective-permute-start | bytes 331784 | tf_op jit(solution)/shard_map/ppermute | solution.py:34
  100.6 4.0 %shard_map.69.inverse = f32[256,256]{1,0:T(8,128)S(1)} custom-call(s32[1]{0:T(128)} %bitcast.1.core, f32[128,256]{1,0:T(8,128)S(1)} %constant_dynamic-update-slice_fusion.mine, f32[128,256]{1,0:T(8,128)S(1)} %collective-permute-done.34.theirs), custom_call_target="tpu_custom_call" | custom-call | flops 3221225472 | bytes 524292 | tf_op jit(solution)/shard_map/pallas_call | solution.py:399
  104.7 1.7 %shard_map.70 = f32[864,256]{1,0:T(8,128)} custom-call(s32[1]{0:T(128)} %bitcast.at, f32[256,256]{1,0:T(8,128)S(1)} %shard_map.69.inverse, bf16[2,32,864]{2,1,0:T(8,128)(2,1)S(1)} %add_convert_fusion.refs_0_, bf16[2,32,864]{2,1,0:T(8,128)(2,1)S(1)} %collective-permute-done.38.refs_1_, bf16[2,32,864]{2,1,0:T(8,128)(2,1)S(1)} %collective-permute-done.39.refs_2_, ...), custom_call_target="tpu_custom_call" | custom-call | flops 679477248 | bytes 1589252 | tf_op jit(solution)/shard_map/pallas_call | solution.py:399
  (99 shorter events, 32.1 us)
Async XLA Ops:
  3.7 20.9 %collective-permute-start.4 = (bf16[384,1024]{1,0:T(8,128)(2,1)S(1)}, bf16[384,1024]{1,0:T(8,128)(2,1)S(1)}, u32[]{:S(2)}, u32[]{:S(2)}) collective-permute-start(bf16[384,1024]{1,0:T(8,128)(2,1)S(1)} %get-tuple-element.33), channel_id=1, source_target_pairs={{0,8},{1,9},{2,10},{3,11},{4,12},{5,13},{6,14},{7,15},{8,0},{9,1},... | collective-permute-start | bytes 2359304 | tf_op jit(solution)/shard_map/ppermute | solution.py:34
  6.8 17.9 %collective-permute-start.5 = (bf16[320,1024]{1,0:T(8,128)(2,1)S(1)}, bf16[320,1024]{1,0:T(8,128)(2,1)S(1)}, u32[]{:S(2)}, u32[]{:S(2)}) collective-permute-start(bf16[320,1024]{1,0:T(8,128)(2,1)S(1)} %get-tuple-element.34), channel_id=1, source_target_pairs={{0,16},{1,17},{2,18},{3,19},{4,20},{5,21},{6,22},{7,23},{8,24},{9,... | collective-permute-start | bytes 1966088 | tf_op jit(solution)/shard_map/ppermute | solution.py:34
  11.2 6.8 %collective-permute-start.1 = (bf16[64,864]{1,0:T(8,128)(2,1)S(1)}, bf16[64,864]{1,0:T(8,128)(2,1)S(1)}, u32[]{:S(2)}, u32[]{:S(2)}) collective-permute-start(bf16[64,864]{1,0:T(8,128)(2,1)S(1)} %maximum_select_fusion.refs_0_), channel_id=1, source_target_pairs={{0,2},{1,3},{2,0},{3,1},{4,6},{5,7},{6,4},{7,5},{8,10},{9,11},{10,... | collective-permute-start | bytes 331784 | tf_op jit(solution)/shard_map/ppermute | solution.py:34
  12.8 11.8 %collective-permute-start.2 = (bf16[64,864]{1,0:T(8,128)(2,1)S(1)}, bf16[64,864]{1,0:T(8,128)(2,1)S(1)}, u32[]{:S(2)}, u32[]{:S(2)}) collective-permute-start(bf16[64,864]{1,0:T(8,128)(2,1)S(1)} %maximum_select_fusion.refs_0_), channel_id=1, source_target_pairs={{0,4},{1,5},{2,6},{3,7},{4,0},{5,1},{6,2},{7,3},{8,12},{9,13},{10,... | collective-permute-start | bytes 331784 | tf_op jit(solution)/shard_map/ppermute | solution.py:34
  15.4 9.3 %collective-permute-start.3 = (bf16[64,864]{1,0:T(8,128)(2,1)S(1)}, bf16[64,864]{1,0:T(8,128)(2,1)S(1)}, u32[]{:S(2)}, u32[]{:S(2)}) collective-permute-start(bf16[64,864]{1,0:T(8,128)(2,1)S(1)} %maximum_select_fusion.refs_0_), channel_id=1, source_target_pairs={{0,6},{1,7},{2,4},{3,5},{4,2},{5,3},{6,0},{7,1},{8,14},{9,15},{10,... | collective-permute-start | bytes 331784 | tf_op jit(solution)/shard_map/ppermute | solution.py:34
  25.7 16.3 %collective-permute-start.9 = (bf16[160,1024]{1,0:T(8,128)(2,1)S(1)}, bf16[160,1024]{1,0:T(8,128)(2,1)S(1)}, u32[]{:S(2)}, u32[]{:S(2)}) collective-permute-start(bf16[160,1024]{1,0:T(8,128)(2,1)S(1)} %get-tuple-element.39), channel_id=1, source_target_pairs={{0,16},{1,17},{2,18},{3,19},{4,20},{5,21},{6,22},{7,23},{8,24},{9,... | collective-permute-start | bytes 983048 | tf_op jit(solution)/shard_map/ppermute | solution.py:34
  27.0 15.1 %collective-permute-start.10 = (bf16[160,1024]{1,0:T(8,128)(2,1)S(1)}, bf16[160,1024]{1,0:T(8,128)(2,1)S(1)}, u32[]{:S(2)}, u32[]{:S(2)}) collective-permute-start(bf16[160,1024]{1,0:T(8,128)(2,1)S(1)} %get-tuple-element.42), channel_id=1, source_target_pairs={{0,8},{1,9},{2,10},{3,11},{4,12},{5,13},{6,14},{7,15},{8,0},{9,1},... | collective-permute-start | bytes 983048 | tf_op jit(solution)/shard_map/ppermute | solution.py:34
  42.6 9.5 %collective-permute-start.13 = (bf16[128,1024]{1,0:T(8,128)(2,1)S(1)}, bf16[128,1024]{1,0:T(8,128)(2,1)S(1)}, u32[]{:S(2)}, u32[]{:S(2)}) collective-permute-start(bf16[128,1024]{1,0:T(8,128)(2,1)S(1)} %get-tuple-element.47), channel_id=1, source_target_pairs={{0,8},{1,9},{2,10},{3,11},{4,12},{5,13},{6,14},{7,15},{8,0},{9,1},... | collective-permute-start | bytes 786440 | tf_op jit(solution)/shard_map/ppermute | solution.py:34
  43.9 13.8 %collective-permute-start.14 = (bf16[128,1024]{1,0:T(8,128)(2,1)S(1)}, bf16[128,1024]{1,0:T(8,128)(2,1)S(1)}, u32[]{:S(2)}, u32[]{:S(2)}) collective-permute-start(bf16[128,1024]{1,0:T(8,128)(2,1)S(1)} %get-tuple-element.40), channel_id=1, source_target_pairs={{0,16},{1,17},{2,18},{3,19},{4,20},{5,21},{6,22},{7,23},{8,24},{9,... | collective-permute-start | bytes 786440 | tf_op jit(solution)/shard_map/ppermute | solution.py:34
  47.5 11.9 %collective-permute-start.15 = (bf16[128,1024]{1,0:T(8,128)(2,1)S(1)}, bf16[128,1024]{1,0:T(8,128)(2,1)S(1)}, u32[]{:S(2)}, u32[]{:S(2)}) collective-permute-start(bf16[128,1024]{1,0:T(8,128)(2,1)S(1)} %get-tuple-element.45.slopes), channel_id=1, source_target_pairs={{0,24},{1,25},{2,26},{3,27},{4,28},{5,29},{6,30},{7,31},{8,16},{9,... | collective-permute-start | bytes 786440 | tf_op jit(solution)/shard_map/ppermute | solution.py:34
  48.5 11.3 %collective-permute-start.22 = (f32[128,256]{1,0:T(8,128)S(1)}, f32[128,256]{1,0:T(8,128)S(1)}, u32[]{:S(2)}, u32[]{:S(2)}) collective-permute-start(f32[128,256]{1,0:T(8,128)S(1)} %get-tuple-element.55), channel_id=1, source_target_pairs={{0,6},{1,7},{2,4},{3,5},{4,2},{5,3},{6,0},{7,1},{8,14},{9,15},{10,... | collective-permute-start | bytes 393224 | tf_op jit(solution)/shard_map/ppermute | solution.py:34
  52.1 11.2 %collective-permute-start.21 = (f32[128,256]{1,0:T(8,128)S(1)}, f32[128,256]{1,0:T(8,128)S(1)}, u32[]{:S(2)}, u32[]{:S(2)}) collective-permute-start(f32[128,256]{1,0:T(8,128)S(1)} %get-tuple-element.55), channel_id=1, source_target_pairs={{0,4},{1,5},{2,6},{3,7},{4,0},{5,1},{6,2},{7,3},{8,12},{9,13},{10,... | collective-permute-start | bytes 393224 | tf_op jit(solution)/shard_map/ppermute | solution.py:34
  52.1 11.2 %collective-permute-start.20 = (f32[128,256]{1,0:T(8,128)S(1)}, f32[128,256]{1,0:T(8,128)S(1)}, u32[]{:S(2)}, u32[]{:S(2)}) collective-permute-start(f32[128,256]{1,0:T(8,128)S(1)} %get-tuple-element.55), channel_id=1, source_target_pairs={{0,2},{1,3},{2,0},{3,1},{4,6},{5,7},{6,4},{7,5},{8,10},{9,11},{10,... | collective-permute-start | bytes 393224 | tf_op jit(solution)/shard_map/ppermute | solution.py:34
  63.9 16.9 %collective-permute-start.30 = (f32[864,256]{1,0:T(8,128)S(1)}, f32[864,256]{1,0:T(8,128)}, u32[]{:S(2)}, u32[]{:S(2)}) collective-permute-start(f32[864,256]{1,0:T(8,128)S(1)} %shard_map.64.mine), channel_id=1, source_target_pairs={{0,1},{1,0},{2,3},{3,2},{4,5},{5,4},{6,7},{7,6},{8,9},{9,8},{10,11... | collective-permute-start | bytes 2654216 | tf_op jit(solution)/shard_map/ppermute | solution.py:34
  65.9 7.6 %collective-permute-start.25 = (f32[32,256]{1,0:T(8,128)S(1)}, f32[32,256]{1,0:T(8,128)S(1)}, u32[]{:S(2)}, u32[]{:S(2)}) collective-permute-start(f32[32,256]{1,0:T(8,128)S(1)} %get-tuple-element.68), channel_id=1, source_target_pairs={{0,24},{1,25},{2,26},{3,27},{4,28},{5,29},{6,30},{7,31},{8,16},{9,... | collective-permute-start | bytes 98312 | tf_op jit(solution)/shard_map/ppermute | solution.py:34
  67.3 6.2 %collective-permute-start.24 = (f32[32,256]{1,0:T(8,128)S(1)}, f32[32,256]{1,0:T(8,128)S(1)}, u32[]{:S(2)}, u32[]{:S(2)}) collective-permute-start(f32[32,256]{1,0:T(8,128)S(1)} %get-tuple-element.69), channel_id=1, source_target_pairs={{0,16},{1,17},{2,18},{3,19},{4,20},{5,21},{6,22},{7,23},{8,24},{9,... | collective-permute-start | bytes 98312 | tf_op jit(solution)/shard_map/ppermute | solution.py:34
  83.0 6.1 %collective-permute-start.31 = (f32[32,256]{1,0:T(8,128)S(1)}, f32[32,256]{1,0:T(8,128)S(1)}, u32[]{:S(2)}, u32[]{:S(2)}) collective-permute-start(f32[32,256]{1,0:T(8,128)S(1)} %add_add_fusion.1), channel_id=1, source_target_pairs={{0,8},{1,9},{2,10},{3,11},{4,12},{5,13},{6,14},{7,15},{8,0},{9,1},... | collective-permute-start | bytes 98312 | tf_op jit(solution)/shard_map/ppermute | solution.py:34
  83.6 7.5 %collective-permute-start.32 = (f32[32,256]{1,0:T(8,128)S(1)}, f32[32,256]{1,0:T(8,128)S(1)}, u32[]{:S(2)}, u32[]{:S(2)}) collective-permute-start(f32[32,256]{1,0:T(8,128)S(1)} %add_add_fusion.1), channel_id=1, source_target_pairs={{0,16},{1,17},{2,18},{3,19},{4,20},{5,21},{6,22},{7,23},{8,24},{9,... | collective-permute-start | bytes 98312 | tf_op jit(solution)/shard_map/ppermute | solution.py:34
  86.6 6.9 %collective-permute-start.37 = (bf16[2,32,864]{2,1,0:T(8,128)(2,1)S(1)}, bf16[2,32,864]{2,1,0:T(8,128)(2,1)S(1)}, u32[]{:S(2)}, u32[]{:S(2)}) collective-permute-start(bf16[2,32,864]{2,1,0:T(8,128)(2,1)S(1)} %get-tuple-element.63), channel_id=1, source_target_pairs={{0,6},{1,7},{2,4},{3,5},{4,2},{5,3},{6,0},{7,1},{8,14},{9,15},{10,... | collective-permute-start | bytes 331784 | tf_op jit(solution)/shard_map/ppermute | solution.py:34
  88.5 8.5 %collective-permute-start.36 = (bf16[2,32,864]{2,1,0:T(8,128)(2,1)S(1)}, bf16[2,32,864]{2,1,0:T(8,128)(2,1)S(1)}, u32[]{:S(2)}, u32[]{:S(2)}) collective-permute-start(bf16[2,32,864]{2,1,0:T(8,128)(2,1)S(1)} %get-tuple-element.64), channel_id=1, source_target_pairs={{0,4},{1,5},{2,6},{3,7},{4,0},{5,1},{6,2},{7,3},{8,12},{9,13},{10,... | collective-permute-start | bytes 331784 | tf_op jit(solution)/shard_map/ppermute | solution.py:34
  89.1 7.9 %collective-permute-start.35 = (bf16[2,32,864]{2,1,0:T(8,128)(2,1)S(1)}, bf16[2,32,864]{2,1,0:T(8,128)(2,1)S(1)}, u32[]{:S(2)}, u32[]{:S(2)}) collective-permute-start(bf16[2,32,864]{2,1,0:T(8,128)(2,1)S(1)} %get-tuple-element.62), channel_id=1, source_target_pairs={{0,2},{1,3},{2,0},{3,1},{4,6},{5,7},{6,4},{7,5},{8,10},{9,11},{10,... | collective-permute-start | bytes 331784 | tf_op jit(solution)/shard_map/ppermute | solution.py:34
  91.1 9.5 %collective-permute-start.34 = (f32[128,256]{1,0:T(8,128)S(1)}, f32[128,256]{1,0:T(8,128)S(1)}, u32[]{:S(2)}, u32[]{:S(2)}) collective-permute-start(f32[128,256]{1,0:T(8,128)S(1)} %constant_dynamic-update-slice_fusion.mine), channel_id=1, source_target_pairs={{0,1},{1,0},{2,3},{3,2},{4,5},{5,4},{6,7},{7,6},{8,9},{9,8},{10,11... | collective-permute-start | bytes 393224 | tf_op jit(solution)/shard_map/ppermute | solution.py:34
  97.0 7.6 %collective-permute-start.38 = (bf16[2,32,864]{2,1,0:T(8,128)(2,1)S(1)}, bf16[2,32,864]{2,1,0:T(8,128)(2,1)S(1)}, u32[]{:S(2)}, u32[]{:S(2)}) collective-permute-start(bf16[2,32,864]{2,1,0:T(8,128)(2,1)S(1)} %add_convert_fusion.refs_0_), channel_id=1, source_target_pairs={{0,8},{1,9},{2,10},{3,11},{4,12},{5,13},{6,14},{7,15},{8,0},{9,1},... | collective-permute-start | bytes 331784 | tf_op jit(solution)/shard_map/ppermute | solution.py:34
  97.6 7.0 %collective-permute-start.39 = (bf16[2,32,864]{2,1,0:T(8,128)(2,1)S(1)}, bf16[2,32,864]{2,1,0:T(8,128)(2,1)S(1)}, u32[]{:S(2)}, u32[]{:S(2)}) collective-permute-start(bf16[2,32,864]{2,1,0:T(8,128)(2,1)S(1)} %add_convert_fusion.refs_0_), channel_id=1, source_target_pairs={{0,16},{1,17},{2,18},{3,19},{4,20},{5,21},{6,22},{7,23},{8,24},{9,... | collective-permute-start | bytes 331784 | tf_op jit(solution)/shard_map/ppermute | solution.py:34
  (23 other events, 85.8 us)

commit v3 on v2

--- a/solution.py
+++ b/solution.py
@@ -566,17 +566,18 @@
         return lax.dynamic_slice_in_dim(array, pair * own_rows, own_rows, 1)
 
     block = part_for(product, my_pair)
-    for step in range(1, pairs):
-        block = block + swap(part_for(narrow, my_pair ^ step), z=step).astype(f32)
+    received = [swap(part_for(narrow, my_pair ^ step), z=step) for step in range(1, pairs)]
+    for part in received:
+        block = block + part.astype(f32)
     g_half = after(g_half, a_half)
     part = rows_of(g_half, my_plane, out)
     for step in range(1, planes):
         part = part + swap(rows_of(g_half, my_plane ^ step, out), dp=step)
-    part = after(part, inv_a)
+    part = after(part, narrow)
     over_z = part
     for step in range(1, pairs):
         over_z = over_z + swap(part, z=step)
-    over_z = after(over_z, narrow)
+    over_z = after(over_z, received[0])
     g_half = jnp.zeros((half, channels), f32)
     for step in range(planes):
         part = over_z if step == 0 else swap(over_z, dp=step)

time: 107 us -> 105 us (0.981)
  starting transfers between devices: 43 us -> 41.9 us
    ppermute x41, starting transfers between devices: 43 us -> 41.9 us  [exchange(): return lax.ppermute(x, AXES, perm)]
  transfers between devices with their start and end apart: 41 -> 41, of which waited for: 12 -> 13; matrix products, arithmetic and copies ran while one was open for 2% -> 2% of each run, Pallas kernels for 25% -> 25%
where the time goes in v3:
time: 105 us
  starting transfers between devices  41.9 us (40%)
  Pallas kernels  31.1 us (30%)
  waiting for transfers between devices  25.7 us (24%)
  local copies, waits for them, and re-layouts  5.14 us (5%)
    ppermute x41, starting transfers between devices, exchange(): return lax.ppermute(x, AXES, perm)  41.9 us
    pallas_call x12, Pallas kernels, call(): pl.pallas_call(kernel, out_shape=tuple(shapes), in_specs=in_specs, out_sp...  31.1 us
    ppermute x41, waiting for transfers between devices, exchange(): return lax.ppermute(x, AXES, perm)  25.7 us
    unnamed x12, local copies, waits for them, and re-layouts  3.17 us
  transfers between devices with their start and end apart: 41, of which 13 were waited for; matrix products, arithmetic and copies ran while one was open for 2% of the time, Pallas kernels for 25%

profile of v3, /device:TPU:0, one launch (start us, length us, event | category | flops | bytes accessed | tf_op | source)
XLA Modules:
  0.0 105.0 jit_solution(8877354393588294614)
XLA Ops:
  3.7 3.0 %collective-permute-start.4 = (bf16[384,1024]{1,0:T(8,128)(2,1)S(1)}, bf16[384,1024]{1,0:T(8,128)(2,1)S(1)}, u32[]{:S(2)}, u32[]{:S(2)}) collective-permute-start(bf16[384,1024]{1,0:T(8,128)(2,1)S(1)} %get-tuple-element.33), channel_id=1, source_target_pairs={{0,8},{1,9},{2,10},{3,11},{4,12},{5,13},{6,14},{7,15},{8,0},{9,1},... | collective-permute-start | bytes 2359304 | tf_op jit(solution)/shard_map/ppermute | solution.py:34
  11.2 1.6 %collective-permute-start.1 = (bf16[64,864]{1,0:T(8,128)(2,1)S(1)}, bf16[64,864]{1,0:T(8,128)(2,1)S(1)}, u32[]{:S(2)}, u32[]{:S(2)}) collective-permute-start(bf16[64,864]{1,0:T(8,128)(2,1)S(1)} %maximum_select_fusion.refs_0_), channel_id=1, source_target_pairs={{0,2},{1,3},{2,0},{3,1},{4,6},{5,7},{6,4},{7,5},{8,10},{9,11},{10,... | collective-permute-start | bytes 331784 | tf_op jit(solution)/shard_map/ppermute | solution.py:34
  12.8 2.6 %collective-permute-start.2 = (bf16[64,864]{1,0:T(8,128)(2,1)S(1)}, bf16[64,864]{1,0:T(8,128)(2,1)S(1)}, u32[]{:S(2)}, u32[]{:S(2)}) collective-permute-start(bf16[64,864]{1,0:T(8,128)(2,1)S(1)} %maximum_select_fusion.refs_0_), channel_id=1, source_target_pairs={{0,4},{1,5},{2,6},{3,7},{4,0},{5,1},{6,2},{7,3},{8,12},{9,13},{10,... | collective-permute-start | bytes 331784 | tf_op jit(solution)/shard_map/ppermute | solution.py:34
  15.6 2.3 %collective-permute-done.1.refs_1_ = bf16[64,864]{1,0:T(8,128)(2,1)S(1)} collective-permute-done((bf16[64,864]{1,0:T(8,128)(2,1)S(1)}, bf16[64,864]{1,0:T(8,128)(2,1)S(1)}, u32[]{:S(2)}, u32[]{:S(2)}) %collective-permute-start.1) | collective-permute-done | bytes 110624 | tf_op jit(solution)/shard_map/ppermute | solution.py:34
  18.0 6.7 %collective-permute-done.2.refs_2_ = bf16[64,864]{1,0:T(8,128)(2,1)S(1)} collective-permute-done((bf16[64,864]{1,0:T(8,128)(2,1)S(1)}, bf16[64,864]{1,0:T(8,128)(2,1)S(1)}, u32[]{:S(2)}, u32[]{:S(2)}) %collective-permute-start.2) | collective-permute-done | bytes 110624 | tf_op jit(solution)/shard_map/ppermute | solution.py:34
  30.2 11.9 %shard_map.61 = (f32[128,256]{1,0:T(8,128)S(1)}, f32[864,256]{1,0:T(8,128)S(1)}, bf16[128,1024]{1,0:T(8,128)(2,1)S(1)}, bf16[128,1024]{1,0:T(8,128)(2,1)S(1)}, bf16[128,1024]{1,0:T(8,128)(2,1)S(1)}) custom-call(s32[1]{0:T(128)} %bitcast.1.core, bf16[288,768]{1,0:T(8,128)(2,1)S(1)} %shard_map.59.kernel, bf16[256,512]{1,0:T(8,128)(2,1)S(1)} %copy-done.5, ...), custom_call_target="tpu_custom_call" | custom-call | flops 5435817984 | bytes 7880708 | tf_op jit(solution)/shard_map/pallas_call | solution.py:399
  45.4 2.0 %shard_map.63 = (f32[128,256]{1,0:T(8,128)S(1)}, bf16[128,1024]{1,0:T(8,128)(2,1)S(1)}) custom-call(s32[1]{0:T(128)} %bitcast.1.core, bf16[288,768]{1,0:T(8,128)(2,1)S(1)} %shard_map.59.kernel, bf16[256,512]{1,0:T(8,128)(2,1)S(1)} %copy-done.5, bf16[160,1024]{1,0:T(8,128)(2,1)S(1)} %collective-permute-done.9.refs_0_, ...), custom_call_target="tpu_custom_call" | custom-call | flops 905969664 | bytes 2539524 | tf_op jit(solution)/shard_map/pallas_call | solution.py:399
  48.5 3.6 %collective-permute-start.22 = (f32[128,256]{1,0:T(8,128)S(1)}, f32[128,256]{1,0:T(8,128)S(1)}, u32[]{:S(2)}, u32[]{:S(2)}) collective-permute-start(f32[128,256]{1,0:T(8,128)S(1)} %get-tuple-element.55), channel_id=1, source_target_pairs={{0,6},{1,7},{2,4},{3,5},{4,2},{5,3},{6,0},{7,1},{8,14},{9,15},{10,... | collective-permute-start | bytes 393224 | tf_op jit(solution)/shard_map/ppermute | solution.py:34
  52.1 1.6 %collective-permute-start.20 = (f32[128,256]{1,0:T(8,128)S(1)}, f32[128,256]{1,0:T(8,128)S(1)}, u32[]{:S(2)}, u32[]{:S(2)}) collective-permute-start(f32[128,256]{1,0:T(8,128)S(1)} %get-tuple-element.55), channel_id=1, source_target_pairs={{0,2},{1,3},{2,0},{3,1},{4,6},{5,7},{6,4},{7,5},{8,10},{9,11},{10,... | collective-permute-start | bytes 393224 | tf_op jit(solution)/shard_map/ppermute | solution.py:34
  53.7 1.6 %shard_map.64.mine = f32[864,256]{1,0:T(8,128)S(1)} custom-call(bf16[256,2304]{1,0:T(8,128)(2,1)S(1)} %copy-done, bf16[128,1024]{1,0:T(8,128)(2,1)S(1)} %get-tuple-element.45.slopes, f32[864,256]{1,0:T(8,128)S(1)} %get-tuple-element.50.total_in, bf16[160,1024]{1,0:T(8,128)(2,1)S(1)} %collective-permute-done.9.refs_0_, ...), custom_call_target="tpu_custom_call", output_to_operand_aliasing={{}: (2, {})} | custom-call | flops 905969664 | bytes 4521984 | tf_op jit(solution)/shard_map/pallas_call | solution.py:399
  55.3 2.3 %collective-permute-done.14.refs_2_ = bf16[128,1024]{1,0:T(8,128)(2,1)S(1)} collective-permute-done((bf16[128,1024]{1,0:T(8,128)(2,1)S(1)}, bf16[128,1024]{1,0:T(8,128)(2,1)S(1)}, u32[]{:S(2)}, u32[]{:S(2)}) %collective-permute-start.14) | collective-permute-done | bytes 262176 | tf_op jit(solution)/shard_map/ppermute | solution.py:34
  58.3 5.1 %collective-permute-done.21 = f32[128,256]{1,0:T(8,128)S(1)} collective-permute-done((f32[128,256]{1,0:T(8,128)S(1)}, f32[128,256]{1,0:T(8,128)S(1)}, u32[]{:S(2)}, u32[]{:S(2)}) %collective-permute-start.21) | collective-permute-done | bytes 131104 | tf_op jit(solution)/shard_map/ppermute | solution.py:34
  69.7 4.0 %shard_map.67.inverse = f32[256,256]{1,0:T(8,128)S(1)} custom-call(s32[1]{0:T(128)} %bitcast.1.core, f32[128,256]{1,0:T(8,128)S(1)} %add_add_fusion.mine, f32[128,256]{1,0:T(8,128)S(1)} %collective-permute-done.26.theirs), custom_call_target="tpu_custom_call" | custom-call | flops 3221225472 | bytes 524292 | tf_op jit(solution)/shard_map/pallas_call | solution.py:399
  73.7 1.6 %shard_map.65 = bf16[256,1024]{1,0:T(8,128)(2,1)} custom-call(s32[1]{0:T(128)} %bitcast.at, s32[1]{0:T(128)} %bitcast.1.core, bf16[128,1024]{1,0:T(8,128)(2,1)S(1)} %get-tuple-element.51.refs_0_, bf16[128,1024]{1,0:T(8,128)(2,1)S(1)} %collective-permute-done.13.refs_1_, bf16[128,1024]{1,0:T(8,128)(2,1)S(1)} %collective-permute-done.14.refs_2_, ...), custom_call_target="tpu_custom_call" | custom-call | bytes 2621448 | tf_op jit(solution)/shard_map/pallas_call | solution.py:399
  75.4 2.1 %shard_map.68 = (f32[2,128,864]{2,1,0:T(8,128)S(1)}, bf16[2,128,864]{2,1,0:T(8,128)(2,1)S(1)}) custom-call(s32[1]{0:T(128)} %bitcast.1.core, f32[256,256]{1,0:T(8,128)S(1)} %shard_map.67.inverse, f32[864,256]{1,0:T(8,128)S(1)} %shard_map.64.mine, f32[864,256]{1,0:T(8,128)} %collective-permute-done.27.theirs), custom_call_target="tpu_custom_call" | custom-call | flops 339738624 | bytes 3358724 | tf_op jit(solution)/shard_map/pallas_call | solution.py:399
  77.5 2.6 %collective-permute-start.30 = (f32[32,256]{1,0:T(8,128)S(1)}, f32[32,256]{1,0:T(8,128)S(1)}, u32[]{:S(2)}, u32[]{:S(2)}) collective-permute-start(f32[32,256]{1,0:T(8,128)S(1)} %add_add_fusion.2), channel_id=1, source_target_pairs={{0,6},{1,7},{2,4},{3,5},{4,2},{5,3},{6,0},{7,1},{8,14},{9,15},{10,... | collective-permute-start | bytes 98312 | tf_op jit(solution)/shard_map/ppermute | solution.py:34
  80.0 1.9 %collective-permute-start.28 = (f32[32,256]{1,0:T(8,128)S(1)}, f32[32,256]{1,0:T(8,128)S(1)}, u32[]{:S(2)}, u32[]{:S(2)}) collective-permute-start(f32[32,256]{1,0:T(8,128)S(1)} %add_add_fusion.2), channel_id=1, source_target_pairs={{0,2},{1,3},{2,0},{3,1},{4,6},{5,7},{6,4},{7,5},{8,10},{9,11},{10,... | collective-permute-start | bytes 98312 | tf_op jit(solution)/shard_map/ppermute | solution.py:34
  82.1 2.4 %collective-permute-start.37 = (bf16[2,32,864]{2,1,0:T(8,128)(2,1)S(1)}, bf16[2,32,864]{2,1,0:T(8,128)(2,1)S(1)}, u32[]{:S(2)}, u32[]{:S(2)}) collective-permute-start(bf16[2,32,864]{2,1,0:T(8,128)(2,1)S(1)} %get-tuple-element.63), channel_id=1, source_target_pairs={{0,6},{1,7},{2,4},{3,5},{4,2},{5,3},{6,0},{7,1},{8,14},{9,15},{10,... | collective-permute-start | bytes 331784 | tf_op jit(solution)/shard_map/ppermute | solution.py:34
  85.5 2.6 %collective-permute-done.31 = bf16[2,32,864]{2,1,0:T(8,128)(2,1)S(1)} collective-permute-done((bf16[2,32,864]{2,1,0:T(8,128)(2,1)S(1)}, bf16[2,32,864]{2,1,0:T(8,128)(2,1)S(1)}, u32[]{:S(2)}, u32[]{:S(2)}) %collective-permute-start.31) | collective-permute-done | bytes 110624 | tf_op jit(solution)/shard_map/ppermute | solution.py:34
  90.0 1.6 %collective-permute-start.34 = (f32[32,256]{1,0:T(8,128)S(1)}, f32[32,256]{1,0:T(8,128)S(1)}, u32[]{:S(2)}, u32[]{:S(2)}) collective-permute-start(f32[32,256]{1,0:T(8,128)S(1)} %add_add_fusion.1), channel_id=1, source_target_pairs={{0,24},{1,25},{2,26},{3,27},{4,28},{5,29},{6,30},{7,31},{8,16},{9,... | collective-permute-start | bytes 98312 | tf_op jit(solution)/shard_map/ppermute | solution.py:34
  92.6 2.3 %collective-permute-done.34 = f32[32,256]{1,0:T(8,128)S(1)} collective-permute-done((f32[32,256]{1,0:T(8,128)S(1)}, f32[32,256]{1,0:T(8,128)S(1)}, u32[]{:S(2)}, u32[]{:S(2)}) %collective-permute-start.34) | collective-permute-done | bytes 32800 | tf_op jit(solution)/shard_map/ppermute | solution.py:34
  95.6 1.6 %collective-permute-start.39 = (bf16[2,32,864]{2,1,0:T(8,128)(2,1)S(1)}, bf16[2,32,864]{2,1,0:T(8,128)(2,1)S(1)}, u32[]{:S(2)}, u32[]{:S(2)}) collective-permute-start(bf16[2,32,864]{2,1,0:T(8,128)(2,1)S(1)} %add_convert_fusion.refs_0_), channel_id=1, source_target_pairs={{0,16},{1,17},{2,18},{3,19},{4,20},{5,21},{6,22},{7,23},{8,24},{9,... | collective-permute-start | bytes 331784 | tf_op jit(solution)/shard_map/ppermute | solution.py:34
  98.5 4.0 %shard_map.69.inverse = f32[256,256]{1,0:T(8,128)S(1)} custom-call(s32[1]{0:T(128)} %bitcast.1.core, f32[128,256]{1,0:T(8,128)S(1)} %constant_dynamic-update-slice_fusion.mine, f32[128,256]{1,0:T(8,128)S(1)} %collective-permute-done.35.theirs), custom_call_target="tpu_custom_call" | custom-call | flops 3221225472 | bytes 524292 | tf_op jit(solution)/shard_map/pallas_call | solution.py:399
  103.3 1.7 %shard_map.70 = f32[864,256]{1,0:T(8,128)} custom-call(s32[1]{0:T(128)} %bitcast.at, f32[256,256]{1,0:T(8,128)S(1)} %shard_map.69.inverse, bf16[2,32,864]{2,1,0:T(8,128)(2,1)S(1)} %add_convert_fusion.refs_0_, bf16[2,32,864]{2,1,0:T(8,128)(2,1)S(1)} %collective-permute-done.38.refs_1_, bf16[2,32,864]{2,1,0:T(8,128)(2,1)S(1)} %collective-permute-done.39.refs_2_, ...), custom_call_target="tpu_custom_call" | custom-call | flops 679477248 | bytes 1589252 | tf_op jit(solution)/shard_map/pallas_call | solution.py:399
  (99 shorter events, 31.4 us)
Async XLA Ops:
  3.7 20.9 %collective-permute-start.4 = (bf16[384,1024]{1,0:T(8,128)(2,1)S(1)}, bf16[384,1024]{1,0:T(8,128)(2,1)S(1)}, u32[]{:S(2)}, u32[]{:S(2)}) collective-permute-start(bf16[384,1024]{1,0:T(8,128)(2,1)S(1)} %get-tuple-element.33), channel_id=1, source_target_pairs={{0,8},{1,9},{2,10},{3,11},{4,12},{5,13},{6,14},{7,15},{8,0},{9,1},... | collective-permute-start | bytes 2359304 | tf_op jit(solution)/shard_map/ppermute | solution.py:34
  6.8 17.9 %collective-permute-start.5 = (bf16[320,1024]{1,0:T(8,128)(2,1)S(1)}, bf16[320,1024]{1,0:T(8,128)(2,1)S(1)}, u32[]{:S(2)}, u32[]{:S(2)}) collective-permute-start(bf16[320,1024]{1,0:T(8,128)(2,1)S(1)} %get-tuple-element.34), channel_id=1, source_target_pairs={{0,16},{1,17},{2,18},{3,19},{4,20},{5,21},{6,22},{7,23},{8,24},{9,... | collective-permute-start | bytes 1966088 | tf_op jit(solution)/shard_map/ppermute | solution.py:34
  11.2 6.8 %collective-permute-start.1 = (bf16[64,864]{1,0:T(8,128)(2,1)S(1)}, bf16[64,864]{1,0:T(8,128)(2,1)S(1)}, u32[]{:S(2)}, u32[]{:S(2)}) collective-permute-start(bf16[64,864]{1,0:T(8,128)(2,1)S(1)} %maximum_select_fusion.refs_0_), channel_id=1, source_target_pairs={{0,2},{1,3},{2,0},{3,1},{4,6},{5,7},{6,4},{7,5},{8,10},{9,11},{10,... | collective-permute-start | bytes 331784 | tf_op jit(solution)/shard_map/ppermute | solution.py:34
  12.8 11.8 %collective-permute-start.2 = (bf16[64,864]{1,0:T(8,128)(2,1)S(1)}, bf16[64,864]{1,0:T(8,128)(2,1)S(1)}, u32[]{:S(2)}, u32[]{:S(2)}) collective-permute-start(bf16[64,864]{1,0:T(8,128)(2,1)S(1)} %maximum_select_fusion.refs_0_), channel_id=1, source_target_pairs={{0,4},{1,5},{2,6},{3,7},{4,0},{5,1},{6,2},{7,3},{8,12},{9,13},{10,... | collective-permute-start | bytes 331784 | tf_op jit(solution)/shard_map/ppermute | solution.py:34
  15.4 9.3 %collective-permute-start.3 = (bf16[64,864]{1,0:T(8,128)(2,1)S(1)}, bf16[64,864]{1,0:T(8,128)(2,1)S(1)}, u32[]{:S(2)}, u32[]{:S(2)}) collective-permute-start(bf16[64,864]{1,0:T(8,128)(2,1)S(1)} %maximum_select_fusion.refs_0_), channel_id=1, source_target_pairs={{0,6},{1,7},{2,4},{3,5},{4,2},{5,3},{6,0},{7,1},{8,14},{9,15},{10,... | collective-permute-start | bytes 331784 | tf_op jit(solution)/shard_map/ppermute | solution.py:34
  25.7 16.3 %collective-permute-start.9 = (bf16[160,1024]{1,0:T(8,128)(2,1)S(1)}, bf16[160,1024]{1,0:T(8,128)(2,1)S(1)}, u32[]{:S(2)}, u32[]{:S(2)}) collective-permute-start(bf16[160,1024]{1,0:T(8,128)(2,1)S(1)} %get-tuple-element.39), channel_id=1, source_target_pairs={{0,16},{1,17},{2,18},{3,19},{4,20},{5,21},{6,22},{7,23},{8,24},{9,... | collective-permute-start | bytes 983048 | tf_op jit(solution)/shard_map/ppermute | solution.py:34
  27.0 15.1 %collective-permute-start.10 = (bf16[160,1024]{1,0:T(8,128)(2,1)S(1)}, bf16[160,1024]{1,0:T(8,128)(2,1)S(1)}, u32[]{:S(2)}, u32[]{:S(2)}) collective-permute-start(bf16[160,1024]{1,0:T(8,128)(2,1)S(1)} %get-tuple-element.42), channel_id=1, source_target_pairs={{0,8},{1,9},{2,10},{3,11},{4,12},{5,13},{6,14},{7,15},{8,0},{9,1},... | collective-permute-start | bytes 983048 | tf_op jit(solution)/shard_map/ppermute | solution.py:34
  42.6 9.5 %collective-permute-start.13 = (bf16[128,1024]{1,0:T(8,128)(2,1)S(1)}, bf16[128,1024]{1,0:T(8,128)(2,1)S(1)}, u32[]{:S(2)}, u32[]{:S(2)}) collective-permute-start(bf16[128,1024]{1,0:T(8,128)(2,1)S(1)} %get-tuple-element.47), channel_id=1, source_target_pairs={{0,8},{1,9},{2,10},{3,11},{4,12},{5,13},{6,14},{7,15},{8,0},{9,1},... | collective-permute-start | bytes 786440 | tf_op jit(solution)/shard_map/ppermute | solution.py:34
  43.9 13.8 %collective-permute-start.14 = (bf16[128,1024]{1,0:T(8,128)(2,1)S(1)}, bf16[128,1024]{1,0:T(8,128)(2,1)S(1)}, u32[]{:S(2)}, u32[]{:S(2)}) collective-permute-start(bf16[128,1024]{1,0:T(8,128)(2,1)S(1)} %get-tuple-element.40), channel_id=1, source_target_pairs={{0,16},{1,17},{2,18},{3,19},{4,20},{5,21},{6,22},{7,23},{8,24},{9,... | collective-permute-start | bytes 786440 | tf_op jit(solution)/shard_map/ppermute | solution.py:34
  47.5 10.2 %collective-permute-start.15 = (bf16[128,1024]{1,0:T(8,128)(2,1)S(1)}, bf16[128,1024]{1,0:T(8,128)(2,1)S(1)}, u32[]{:S(2)}, u32[]{:S(2)}) collective-permute-start(bf16[128,1024]{1,0:T(8,128)(2,1)S(1)} %get-tuple-element.45.slopes), channel_id=1, source_target_pairs={{0,24},{1,25},{2,26},{3,27},{4,28},{5,29},{6,30},{7,31},{8,16},{9,... | collective-permute-start | bytes 786440 | tf_op jit(solution)/shard_map/ppermute | solution.py:34
  48.5 9.6 %collective-permute-start.22 = (f32[128,256]{1,0:T(8,128)S(1)}, f32[128,256]{1,0:T(8,128)S(1)}, u32[]{:S(2)}, u32[]{:S(2)}) collective-permute-start(f32[128,256]{1,0:T(8,128)S(1)} %get-tuple-element.55), channel_id=1, source_target_pairs={{0,6},{1,7},{2,4},{3,5},{4,2},{5,3},{6,0},{7,1},{8,14},{9,15},{10,... | collective-permute-start | bytes 393224 | tf_op jit(solution)/shard_map/ppermute | solution.py:34
  52.1 11.2 %collective-permute-start.21 = (f32[128,256]{1,0:T(8,128)S(1)}, f32[128,256]{1,0:T(8,128)S(1)}, u32[]{:S(2)}, u32[]{:S(2)}) collective-permute-start(f32[128,256]{1,0:T(8,128)S(1)} %get-tuple-element.55), channel_id=1, source_target_pairs={{0,4},{1,5},{2,6},{3,7},{4,0},{5,1},{6,2},{7,3},{8,12},{9,13},{10,... | collective-permute-start | bytes 393224 | tf_op jit(solution)/shard_map/ppermute | solution.py:34
  52.1 11.2 %collective-permute-start.20 = (f32[128,256]{1,0:T(8,128)S(1)}, f32[128,256]{1,0:T(8,128)S(1)}, u32[]{:S(2)}, u32[]{:S(2)}) collective-permute-start(f32[128,256]{1,0:T(8,128)S(1)} %get-tuple-element.55), channel_id=1, source_target_pairs={{0,2},{1,3},{2,0},{3,1},{4,6},{5,7},{6,4},{7,5},{8,10},{9,11},{10,... | collective-permute-start | bytes 393224 | tf_op jit(solution)/shard_map/ppermute | solution.py:34
  57.7 6.2 %collective-permute-start.16 = (bf16[128,1024]{1,0:T(8,128)(2,1)S(1)}, bf16[128,1024]{1,0:T(8,128)(2,1)S(1)}, u32[]{:S(2)}, u32[]{:S(2)}) collective-permute-start(bf16[128,1024]{1,0:T(8,128)(2,1)S(1)} %get-tuple-element.51.refs_0_), channel_id=1, source_target_pairs={{0,1},{1,0},{2,3},{3,2},{4,5},{5,4},{6,7},{7,6},{8,9},{9,8},{10,11... | collective-permute-start | bytes 786440 | tf_op jit(solution)/shard_map/ppermute | solution.py:34
  57.7 6.3 %collective-permute-start.17 = (bf16[128,1024]{1,0:T(8,128)(2,1)S(1)}, bf16[128,1024]{1,0:T(8,128)(2,1)S(1)}, u32[]{:S(2)}, u32[]{:S(2)}) collective-permute-start(bf16[128,1024]{1,0:T(8,128)(2,1)S(1)} %collective-permute-done.13.refs_1_), channel_id=1, source_target_pairs={{0,1},{1,0},{2,3},{3,2},{4,5},{5,4},{6,7},{7,6},{8,9},{9,8},{10,11... | collective-permute-start | bytes 786440 | tf_op jit(solution)/shard_map/ppermute | solution.py:34
  63.3 12.0 %collective-permute-start.27 = (f32[864,256]{1,0:T(8,128)S(1)}, f32[864,256]{1,0:T(8,128)}, u32[]{:S(2)}, u32[]{:S(2)}) collective-permute-start(f32[864,256]{1,0:T(8,128)S(1)} %shard_map.64.mine), channel_id=1, source_target_pairs={{0,1},{1,0},{2,3},{3,2},{4,5},{5,4},{6,7},{7,6},{8,9},{9,8},{10,11... | collective-permute-start | bytes 2654216 | tf_op jit(solution)/shard_map/ppermute | solution.py:34
  66.2 9.1 %collective-permute-start.25 = (f32[32,256]{1,0:T(8,128)S(1)}, f32[32,256]{1,0:T(8,128)S(1)}, u32[]{:S(2)}, u32[]{:S(2)}) collective-permute-start(f32[32,256]{1,0:T(8,128)S(1)} %get-tuple-element.68), channel_id=1, source_target_pairs={{0,24},{1,25},{2,26},{3,27},{4,28},{5,29},{6,30},{7,31},{8,16},{9,... | collective-permute-start | bytes 98312 | tf_op jit(solution)/shard_map/ppermute | solution.py:34
  67.6 7.7 %collective-permute-start.24 = (f32[32,256]{1,0:T(8,128)S(1)}, f32[32,256]{1,0:T(8,128)S(1)}, u32[]{:S(2)}, u32[]{:S(2)}) collective-permute-start(f32[32,256]{1,0:T(8,128)S(1)} %get-tuple-element.69), channel_id=1, source_target_pairs={{0,16},{1,17},{2,18},{3,19},{4,20},{5,21},{6,22},{7,23},{8,24},{9,... | collective-permute-start | bytes 98312 | tf_op jit(solution)/shard_map/ppermute | solution.py:34
  68.2 7.1 %collective-permute-start.23 = (f32[32,256]{1,0:T(8,128)S(1)}, f32[32,256]{1,0:T(8,128)S(1)}, u32[]{:S(2)}, u32[]{:S(2)}) collective-permute-start(f32[32,256]{1,0:T(8,128)S(1)} %get-tuple-element.67), channel_id=1, source_target_pairs={{0,8},{1,9},{2,10},{3,11},{4,12},{5,13},{6,14},{7,15},{8,0},{9,1},... | collective-permute-start | bytes 98312 | tf_op jit(solution)/shard_map/ppermute | solution.py:34
  77.5 7.1 %collective-permute-start.30 = (f32[32,256]{1,0:T(8,128)S(1)}, f32[32,256]{1,0:T(8,128)S(1)}, u32[]{:S(2)}, u32[]{:S(2)}) collective-permute-start(f32[32,256]{1,0:T(8,128)S(1)} %add_add_fusion.2), channel_id=1, source_target_pairs={{0,6},{1,7},{2,4},{3,5},{4,2},{5,3},{6,0},{7,1},{8,14},{9,15},{10,... | collective-permute-start | bytes 98312 | tf_op jit(solution)/shard_map/ppermute | solution.py:34
  82.1 12.7 %collective-permute-start.37 = (bf16[2,32,864]{2,1,0:T(8,128)(2,1)S(1)}, bf16[2,32,864]{2,1,0:T(8,128)(2,1)S(1)}, u32[]{:S(2)}, u32[]{:S(2)}) collective-permute-start(bf16[2,32,864]{2,1,0:T(8,128)(2,1)S(1)} %get-tuple-element.63), channel_id=1, source_target_pairs={{0,6},{1,7},{2,4},{3,5},{4,2},{5,3},{6,0},{7,1},{8,14},{9,15},{10,... | collective-permute-start | bytes 331784 | tf_op jit(solution)/shard_map/ppermute | solution.py:34
  84.6 10.3 %collective-permute-start.36 = (bf16[2,32,864]{2,1,0:T(8,128)(2,1)S(1)}, bf16[2,32,864]{2,1,0:T(8,128)(2,1)S(1)}, u32[]{:S(2)}, u32[]{:S(2)}) collective-permute-start(bf16[2,32,864]{2,1,0:T(8,128)(2,1)S(1)} %get-tuple-element.62), channel_id=1, source_target_pairs={{0,4},{1,5},{2,6},{3,7},{4,0},{5,1},{6,2},{7,3},{8,12},{9,13},{10,... | collective-permute-start | bytes 331784 | tf_op jit(solution)/shard_map/ppermute | solution.py:34
  94.9 7.6 %collective-permute-start.38 = (bf16[2,32,864]{2,1,0:T(8,128)(2,1)S(1)}, bf16[2,32,864]{2,1,0:T(8,128)(2,1)S(1)}, u32[]{:S(2)}, u32[]{:S(2)}) collective-permute-start(bf16[2,32,864]{2,1,0:T(8,128)(2,1)S(1)} %add_convert_fusion.refs_0_), channel_id=1, source_target_pairs={{0,8},{1,9},{2,10},{3,11},{4,12},{5,13},{6,14},{7,15},{8,0},{9,1},... | collective-permute-start | bytes 331784 | tf_op jit(solution)/shard_map/ppermute | solution.py:34
  95.6 7.7 %collective-permute-start.39 = (bf16[2,32,864]{2,1,0:T(8,128)(2,1)S(1)}, bf16[2,32,864]{2,1,0:T(8,128)(2,1)S(1)}, u32[]{:S(2)}, u32[]{:S(2)}) collective-permute-start(bf16[2,32,864]{2,1,0:T(8,128)(2,1)S(1)} %add_convert_fusion.refs_0_), channel_id=1, source_target_pairs={{0,16},{1,17},{2,18},{3,19},{4,20},{5,21},{6,22},{7,23},{8,24},{9,... | collective-permute-start | bytes 331784 | tf_op jit(solution)/shard_map/ppermute | solution.py:34
  (23 other events, 84.8 us)
